TPU v7x, 256 devices: a whole 4x4x8 slice. The times are simulated.
256 devices in a mesh: tile: 64 (over y, z, core), depth: 4 (over x).
Axes of the slice: x: 4, y: 4, z: 8, core: 2. Of those that a mesh axis runs over, the one named last changes fastest.
Arguments:
- object_real: float32 [12, 8192, 256], P('depth', 'tile'), may hold values from 0.75 to 1.05
- object_imag: float32 [12, 8192, 256], P('depth', 'tile'), may hold values from -0.3 to 0.3
- probe_real: float32 [2, 128, 128], replicated, may hold values from -3 to 3
- probe_imag: float32 [2, 128, 128], replicated, may hold values from -3 to 3
- measured: float32 [256, 128, 128], P('tile'), may hold values from 0 to 1.2
- row_offset: int32 [256], P('tile'), may hold values from 0 to 127
- col_offset: int32 [256], P('tile'), may hold values from 0 to 128
- counts: int32 [64], replicated, may hold values from 1 to 4, as said below
Outputs:
- new_object_real: float32 [12, 8192, 256], P('depth', 'tile')
- new_object_imag: float32 [12, 8192, 256], P('depth', 'tile')
- new_probe_real: float32 [2, 128, 128], P(None, 'depth')
- new_probe_imag: float32 [2, 128, 128], P(None, 'depth')
Inputs may be any that keep to these rules, and one draw needn't show every extreme that they name: `counts`: live positions of each tile; 4 on at least one tile.
All inputs are finite; a program needn't handle non-finite values.
Results may differ from a plain program's by a relative error of at most 0.0003.
Values sent between devices are 32-bit elements; how exact they have to be, the bound alone decides.
A program may use at most 128 MiB of HBM per device.

v0:
```python
import jax
import jax.numpy as jnp
from jax import lax
from jax.sharding import PartitionSpec as P

PRECISE = lax.Precision.HIGHEST
PROP_PHASE = 12.0
AMP_EPS = 0.05
OBJ_STEP = 1.0
PROBE_STEP = 4.0


def shifted(block, axis, distance):
    devices = range(lax.axis_size(axis))
    route = [((i - distance) % len(devices), i) for i in devices]
    return lax.ppermute(block, axis, route)


def passed_along(block, axis, distance):
    devices = range(lax.axis_size(axis))
    route = [(i - distance, i) for i in devices if i - distance in devices]
    return lax.ppermute(block, axis, route)


def broadcast(shard, axis, root):
    mine = lax.axis_index(axis) == root
    return lax.psum(jnp.where(mine, shard, jnp.zeros_like(shard)), axis)


def make_tables(length):
    positions = jnp.arange(length, dtype=jnp.int32)
    product = positions[:, None] * positions[None, :] % length
    angles = -2.0 * jnp.pi / length * product.astype(jnp.float32)
    scale_factor = 1.0 / jnp.sqrt(jnp.float32(length))
    frequency = ((positions + length // 2) % length - length // 2).astype(jnp.float32) / length
    phases = PROP_PHASE * (frequency[:, None] ** 2 + frequency[None, :] ** 2)
    return (
        jnp.cos(angles) * scale_factor,
        jnp.sin(angles) * scale_factor,
        jnp.cos(phases),
        -jnp.sin(phases),
    )


def left_apply(dft_real, dft_imag, field_real, field_imag):
    real_real = jnp.einsum("kn,...nm->...km", dft_real, field_real, precision=PRECISE)
    imag_imag = jnp.einsum("kn,...nm->...km", dft_imag, field_imag, precision=PRECISE)
    real_imag = jnp.einsum("kn,...nm->...km", dft_real, field_imag, precision=PRECISE)
    imag_real = jnp.einsum("kn,...nm->...km", dft_imag, field_real, precision=PRECISE)
    return (real_real - imag_imag, real_imag + imag_real)


def right_apply(dft_real, dft_imag, field_real, field_imag):
    real_real = jnp.einsum("...nm,ml->...nl", field_real, dft_real, precision=PRECISE)
    imag_imag = jnp.einsum("...nm,ml->...nl", field_imag, dft_imag, precision=PRECISE)
    real_imag = jnp.einsum("...nm,ml->...nl", field_real, dft_imag, precision=PRECISE)
    imag_real = jnp.einsum("...nm,ml->...nl", field_imag, dft_real, precision=PRECISE)
    return (real_real - imag_imag, real_imag + imag_real)


def transform(field_real, field_imag, dft_real, dft_imag):
    middle_real, middle_imag = left_apply(dft_real, dft_imag, field_real, field_imag)
    return right_apply(dft_real, dft_imag, middle_real, middle_imag)


def propagate(wavefield, tables, flip_sign):
    dft_real, dft_imag, kern_real, kern_imag = tables
    spec_real, spec_imag = transform(wavefield[0], wavefield[1], dft_real, dft_imag)
    kern_imag = flip_sign * kern_imag
    mixed_real = kern_real * spec_real - kern_imag * spec_imag
    mixed_imag = kern_real * spec_imag + kern_imag * spec_real
    back_real, back_imag = transform(mixed_real, mixed_imag, dft_real, -dft_imag)
    return jnp.stack([back_real, back_imag])


def forward_section(wavefield, patches, is_final, tables):
    levels = patches.shape[2]
    stored = []
    for level in range(levels):
        stored.append(wavefield)
        patch_real = patches[0][:, level][:, None]
        patch_imag = patches[1][:, level][:, None]
        product = jnp.stack(
            [
                wavefield[0] * patch_real - wavefield[1] * patch_imag,
                wavefield[0] * patch_imag + wavefield[1] * patch_real,
            ]
        )
        if level == levels - 1:
            wavefield = lax.cond(
                is_final, lambda given: given, lambda given: propagate(given, tables, 1.0), product
            )
        else:
            wavefield = propagate(product, tables, 1.0)
    return (wavefield, jnp.stack(stored))


def backward_section(gradient, stored, patches, is_final, tables):
    levels = patches.shape[2]
    pieces = [None] * levels
    for level in reversed(range(levels)):
        if level == levels - 1:
            product_grad = lax.cond(
                is_final,
                lambda given: given,
                lambda given: propagate(given, tables, -1.0),
                gradient,
            )
        else:
            product_grad = propagate(gradient, tables, -1.0)
        wave_real = stored[level][0]
        wave_imag = stored[level][1]
        piece_real = jnp.sum(wave_real * product_grad[0] + wave_imag * product_grad[1], axis=1)
        piece_imag = jnp.sum(wave_real * product_grad[1] - wave_imag * product_grad[0], axis=1)
        pieces[level] = jnp.stack([piece_real, piece_imag])
        patch_real = patches[0][:, level][:, None]
        patch_imag = patches[1][:, level][:, None]
        gradient = jnp.stack(
            [
                patch_real * product_grad[0] + patch_imag * product_grad[1],
                patch_real * product_grad[1] - patch_imag * product_grad[0],
            ]
        )
    return (gradient, jnp.stack(pieces, axis=2))


def far_gradient(exit_wave, measured, live_mask, tables):
    dft_real, dft_imag = (tables[0], tables[1])
    spec_real, spec_imag = transform(exit_wave[0], exit_wave[1], dft_real, dft_imag)
    intensity = jnp.sum(spec_real * spec_real + spec_imag * spec_imag, axis=1)
    amplitude = jnp.sqrt(intensity + AMP_EPS)
    factor = ((1.0 - measured / amplitude) * live_mask[:, None, None])[:, None]
    back_real, back_imag = transform(spec_real * factor, spec_imag * factor, dft_real, -dft_imag)
    return jnp.stack([back_real, back_imag])


def body(
    object_real, object_imag, probe_real, probe_imag, measured, row_offset, col_offset, counts
):
    slices_dev, rows_dev, cols_dev = object_real.shape
    pixels = measured.shape[-1]
    slot_count = row_offset.shape[0]
    tables = make_tables(pixels)
    depth_index = lax.axis_index("depth")
    depth_count = lax.axis_size("depth")
    is_final = depth_index == depth_count - 1
    objects = jnp.stack([object_real, object_imag])
    head_rows = shifted(objects, "tile", -1)
    extended = jnp.concatenate([objects, head_rows], axis=2)

    def cut_patch(row_start, col_start):
        return lax.dynamic_slice(
            extended, (0, 0, row_start, col_start), (2, slices_dev, pixels, pixels)
        )

    patches = jnp.moveaxis(jax.vmap(cut_patch)(row_offset, col_offset), 0, 1)
    own_count = lax.dynamic_index_in_dim(counts, lax.axis_index("tile"), 0, keepdims=False)
    live_mask = (jnp.arange(slot_count) < own_count).astype(jnp.float32)
    probe_field = jnp.stack([probe_real, probe_imag])
    wave_shape = probe_field.shape[1:]
    wavefield = jnp.broadcast_to(probe_field[:, None], (2, slot_count) + wave_shape)
    stored = jnp.zeros((slices_dev, 2, slot_count) + wave_shape, jnp.float32)
    outgoing = wavefield
    for section_step in range(depth_count):

        def run_forward(args_in):
            return forward_section(args_in[0], patches, is_final, tables)

        outgoing, stored = lax.cond(
            depth_index == section_step, run_forward, lambda args_in: args_in, (wavefield, stored)
        )
        if section_step < depth_count - 1:
            wavefield = passed_along(outgoing, "depth", 1)
    gradient = lax.cond(
        is_final,
        lambda given: far_gradient(given, measured, live_mask, tables),
        lambda given: jnp.zeros_like(given),
        outgoing,
    )
    patch_grad = jnp.zeros_like(patches)
    returned = gradient
    for section_step in reversed(range(depth_count)):

        def run_backward(args_in):
            return backward_section(args_in[0], stored, patches, is_final, tables)

        returned, patch_grad = lax.cond(
            depth_index == section_step,
            run_backward,
            lambda args_in: args_in,
            (gradient, patch_grad),
        )
        if section_step > 0:
            gradient = passed_along(returned, "depth", -1)
    probe_grad = jnp.sum(returned, axis=1)

    def add_member(member, accum):
        row_start = row_offset[member]
        col_start = col_offset[member]
        piece = lax.dynamic_index_in_dim(patch_grad, member, 1, keepdims=False)
        block = lax.dynamic_slice(
            accum, (0, 0, row_start, col_start), (2, slices_dev, pixels, pixels)
        )
        return lax.dynamic_update_slice(accum, block + piece, (0, 0, row_start, col_start))

    extended_grad = lax.fori_loop(0, slot_count, add_member, jnp.zeros_like(extended))
    received = shifted(extended_grad[:, :, rows_dev:], "tile", 1)
    object_grad = jnp.concatenate(
        [extended_grad[:, :, :pixels] + received, extended_grad[:, :, pixels:rows_dev]], axis=2
    )
    tile_total = lax.psum(probe_grad, "tile")
    probe_total = broadcast(tile_total, "depth", 0)
    probe_rows = pixels // depth_count
    probe_begin = depth_index * probe_rows
    grad_mine = lax.dynamic_slice_in_dim(probe_total, probe_begin, probe_rows, 2)
    real_mine = lax.dynamic_slice_in_dim(probe_real, probe_begin, probe_rows, 1)
    imag_mine = lax.dynamic_slice_in_dim(probe_imag, probe_begin, probe_rows, 1)
    live_total = jnp.sum(counts).astype(jnp.float32)
    return (
        object_real - OBJ_STEP * object_grad[0],
        object_imag - OBJ_STEP * object_grad[1],
        real_mine - PROBE_STEP * grad_mine[0] / live_total,
        imag_mine - PROBE_STEP * grad_mine[1] / live_total,
    )


def solution(mesh):
    placed = (
        P("depth", "tile", None),
        P("depth", "tile", None),
        P(),
        P(),
        P("tile", None, None),
        P("tile"),
        P("tile"),
        P(),
    )
    return jax.shard_map(
        body,
        mesh=mesh,
        in_specs=placed,
        out_specs=(
            P("depth", "tile", None),
            P("depth", "tile", None),
            P(None, "depth", None),
            P(None, "depth", None),
        ),
        check_vma=False,
    )
```

profile of v0, /device:TPU:8, one launch (start us, length us, event | category | flops | bytes accessed | tf_op | source)
XLA Modules:
  0.0 979.4 jit_solution(11495792396357325337)
XLA Ops:
  9.4 5.2 collective-permute-start
  16.4 8.0 collective-permute-done
  27.0 13.0 %while.15 = (s32[]{:T(128)}, f32[2,3,256,256]{3,2,1,0:T(8,128)}, s32[4,4]{1,0:T(4,128)S(1)}, f32[4,2,3,128,128]{4,3,2,1,0:T(8,128)S(1)}, s32[]{:T(128)}) while((s32[]{:T(128)}, f32[2,3,256,256]{3,2,1,0:T(8,128)}, s32[4,4]{1,0:T(4,128)S(1)}, f32[4,2,3,128,128]{4,3,2,1,0:T(8,128)S(1)}, s32[]{:T(128)}) %tuple.369), condition=%wide.while_cond, body=%wide.while_body.sunk | while | flops 2 | bytes 786557 | solution.py:152
  30.9 2.6 bitcast_dynamic-update-slice_fusion.2
  34.1 2.6 bitcast_dynamic-update-slice_fusion.2
  40.0 64.8 %conditional.17 = (f32[2,4,2,128,128]{4,3,2,1,0:T(8,128)}, f32[3,2,4,2,128,128]{5,4,3,2,1,0:T(8,128)}) conditional(s32[]{:T(128)} %convert_element_type.1049, (f32[2,4,2,128,128]{3,4,2,1,0:T(8,128)S(1)}) %tuple.205, (pred[]{:T(512)}, f32[128,128]{1,0:T(8,128)S(1)}, f32[128,128]{1,0:T(8,128)S(1)}, f32[128,128]{1,0:T(8,128)S(1)}, ...), branch_computations={%region_0.1_spmd, %region_1.4_spmd} | conditional | flops 9678290944 | bytes 112984408 | solution.py:169
  78.2 17.8 %conditional = (f32[2,4,2,128,128]{4,3,2,1,0:T(8,128)}) conditional(s32[]{:T(128)} %convert_element_type.10, (f32[128,128]{1,0:T(8,128)S(1)}, f32[128,128]{1,0:T(8,128)S(1)}, f32[4,2,128,128]{3,2,1,0:T(8,128)S(1)}, f32[128,128]{1,0:T(8,128)S(1)}, f32[4,2,128,128]{3,2,1,0:T(8,128)S(1)}, /*index=5*/f32[128,128]{1,0:T(8,128)S(1)}, ...), branch_computations={%region_2.2_spmd, %region_3.3_spmd} | conditional | flops 3224174592 | bytes 26738696 | solution.py:90
  107.2 19.2 %collective-permute-done.1 = f32[2,4,2,128,128]{4,3,2,1,0:T(8,128)} collective-permute-done((f32[2,4,2,128,128]{4,3,2,1,0:T(8,128)}, f32[2,4,2,128,128]{4,3,2,1,0:T(8,128)}, u32[]{:S(2)}, u32[]{:S(2)}) %collective-permute-start.1) | collective-permute-done | bytes 1048608 | tf_op jit(solution)/shard_map/ppermute | solution.py:22
  126.3 8.8 conditional.18
  135.1 65.5 %collective-permute-start.2 = (f32[2,4,2,128,128]{4,3,2,1,0:T(8,128)}, f32[2,4,2,128,128]{4,3,2,1,0:T(8,128)}, u32[]{:S(2)}, u32[]{:S(2)}) collective-permute-start(f32[2,4,2,128,128]{4,3,2,1,0:T(8,128)} %get-tuple-element.1748), channel_id=1, source_target_pairs={{0,1},{1,2},{2,3},{4,5},{5,6},{6,7},{8,9},{9,10},{10,11},{12,13},{... | collective-permute-start | bytes 3145736 | tf_op jit(solution)/shard_map/ppermute | solution.py:22
  200.6 18.3 %collective-permute-done.2 = f32[2,4,2,128,128]{4,3,2,1,0:T(8,128)} collective-permute-done((f32[2,4,2,128,128]{4,3,2,1,0:T(8,128)}, f32[2,4,2,128,128]{4,3,2,1,0:T(8,128)}, u32[]{:S(2)}, u32[]{:S(2)}) %collective-permute-start.2) | collective-permute-done | bytes 1048608 | tf_op jit(solution)/shard_map/ppermute | solution.py:22
  218.9 8.8 conditional.19
  227.7 4.5 collective-permute-start.3
  233.5 17.0 %collective-permute-done.3 = f32[2,4,2,128,128]{4,3,2,1,0:T(8,128)S(1)} collective-permute-done((f32[2,4,2,128,128]{4,3,2,1,0:T(8,128)}, f32[2,4,2,128,128]{4,3,2,1,0:T(8,128)S(1)}, u32[]{:S(2)}, u32[]{:S(2)}) %collective-permute-start.3) | collective-permute-done | bytes 1048608 | tf_op jit(solution)/shard_map/ppermute | solution.py:22
  250.5 8.6 conditional.20
  259.1 11.4 %conditional.21 = (f32[2,4,2,128,128]{4,3,2,1,0:T(8,128)}) conditional(s32[]{:T(128)} %convert_element_type.1052, () %tuple.166, (f32[2,4,2,128,128]{4,3,2,1,0:T(8,128)S(1)}, f32[128,128]{1,0:T(8,128)S(1)}, f32[128,128]{1,0:T(8,128)S(1)}, f32[128,128]{1,0:T(8,128)S(1)}, f32[128,128]{1,0:T(8,128)S(1)}, /*index=5*/f32[128,128]{1,0:T(8,128)S(1)}, ...), branch_computations={%region_16.17_spmd, %region_17.19_spmd} | conditional | flops 3223846912 | bytes 34078800 | solution.py:174
  270.5 11.2 %conditional.22 = (f32[2,4,2,128,128]{4,3,2,1,0:T(8,128)}, f32[2,4,3,128,128]{4,3,1,0,2:T(8,128)}) conditional(s32[]{:T(128)} %convert_element_type.1052, f32[2,4,2,128,128]{4,3,2,1,0:T(8,128)} %get-tuple-element.2855, (f32[2,4,3,128,128]{4,3,2,0,1:T(8,128)S(1)}, f32[128,128]{1,0:T(8,128)S(1)}, f32[128,128]{1,0:T(8,128)S(1)}, ...), branch_computations={%region_19.20_spmd, %region_20.29_spmd} | conditional | flops 9679962112 | bytes 112460088 | solution.py:187
  283.0 79.7 %collective-permute-done.4 = f32[2,4,2,128,128]{4,3,2,1,0:T(8,128)} collective-permute-done((f32[2,4,2,128,128]{4,3,2,1,0:T(8,128)}, f32[2,4,2,128,128]{4,3,2,1,0:T(8,128)}, u32[]{:S(2)}, u32[]{:S(2)}) %collective-permute-start.4) | collective-permute-done | bytes 1048608 | tf_op jit(solution)/shard_map/ppermute | solution.py:22
  362.6 9.0 conditional.23
  373.0 20.8 %collective-permute-done.5 = f32[2,4,2,128,128]{4,3,2,1,0:T(8,128)} collective-permute-done((f32[2,4,2,128,128]{4,3,2,1,0:T(8,128)}, f32[2,4,2,128,128]{4,3,2,1,0:T(8,128)}, u32[]{:S(2)}, u32[]{:S(2)}) %collective-permute-start.5) | collective-permute-done | bytes 1048608 | tf_op jit(solution)/shard_map/ppermute | solution.py:22
  393.8 8.9 conditional.24
  404.0 216.9 %collective-permute-done.6 = f32[2,4,2,128,128]{4,3,2,1,0:T(8,128)S(1)} collective-permute-done((f32[2,4,2,128,128]{4,3,2,1,0:T(8,128)}, f32[2,4,2,128,128]{4,3,2,1,0:T(8,128)S(1)}, u32[]{:S(2)}, u32[]{:S(2)}) %collective-permute-start.6) | collective-permute-done | bytes 1048608 | tf_op jit(solution)/shard_map/ppermute | solution.py:22
  620.9 58.7 %conditional.25 = (f32[2,4,2,128,128]{4,3,2,1,0:T(8,128)S(1)}, f32[2,4,3,128,128]{4,3,2,0,1:T(8,128)S(1)}) conditional(s32[]{:T(128)} %convert_element_type.1049, (f32[2,4,2,128,128]{4,3,2,1,0:T(8,128)S(1)}, f32[2,4,3,128,128]{4,3,1,0,2:T(8,128)}) %tuple.180, (f32[2,4,3,128,128]{4,3,2,0,1:T(8,128)S(1)}, f32[128,128]{1,0:T(8,128)S(1)}, ...), branch_computations={%region_49.50_spmd, %region_50.59_spmd} | conditional | flops 9679962112 | bytes 113508616 | solution.py:187
  621.9 21.3 %conditional.7 = (f32[4,2,128,128]{3,2,1,0:T(8,128)S(1)}, f32[4,2,128,128]{3,2,1,0:T(8,128)S(1)}) conditional(s32[]{:T(128)} %convert_element_type.20, (f32[128,128]{1,0:T(8,128)S(1)}, f32[128,128]{1,0:T(8,128)S(1)}, f32[2,4,2,128,128]{4,3,2,1,0:T(8,128)S(1)}, f32[128,128]{1,0:T(8,128)S(1)}, f32[128,128]{1,0:T(8,128)S(1)}, ...), branch_computations={%region_51.51_spmd, %region_52.52_spmd} | conditional | flops 3223945216 | bytes 27000848 | solution.py:103
  675.2 3.5 fusion.831
  681.4 41.8 %while.14 = (s32[]{:T(128)}, f32[2,3,256,256]{3,2,1,0:T(8,128)S(1)}, s32[4]{0:T(128)S(1)}, s32[4]{0:T(128)S(1)}, f32[2,4,3,128,128]{4,3,2,0,1:T(8,128)}, /*index=5*/s32[]{:T(128)}, s32[]{:T(128)}, s32[]{:T(128)}) while((s32[]{:T(128)}, f32[2,3,256,256]{3,2,1,0:T(8,128)S(1)}, s32[4]{0:T(128)S(1)}, s32[4]{0:T(128)S(1)}, ...), condition=%wide.region_60.61_spmd, body=%wide.region_59.60_spmd.sunk | while | flops 98312 | bytes 1966273 | solution.py:206
  687.7 4.1 dynamic_update_slice.8
  698.1 4.2 dynamic_update_slice.8
  708.5 4.2 dynamic_update_slice.8
  719.0 4.3 dynamic_update_slice.8
  725.2 195.0 %all-reduce.3.cloned.1.call-done = f32[2,2,128,128]{3,2,1,0:T(8,128)} async-done(((f32[2,2,128,128]{3,2,1,0:T(8,128)}), f32[2,2,128,128]{3,2,1,0:T(8,128)}) %all-reduce.3.cloned.1.call-update) | async-done | bytes 262160 | tf_op jit(solution)/shard_map/psum | solution.py:211
  923.2 45.6 %all-reduce.5.cloned.1.call-done = f32[2,2,128,128]{3,2,1,0:T(8,128)} async-done(((f32[2,2,128,128]{3,2,1,0:T(8,128)}), f32[2,2,128,128]{3,2,1,0:T(8,128)}) %all-reduce.5.cloned.1.call-update) | async-done | bytes 262160 | tf_op jit(solution)/shard_map/psum | solution.py:27
  (216 shorter events, 146.1 us)
Async XLA Ops:
  7.2 7.5 copy-start.36
  7.2 7.5 copy-start.38
  7.2 7.6 copy-start.35
  7.2 7.6 copy-start.34
  7.2 913.0 %all-reduce.3.cloned.1.call-start = ((), (), s32[]{:S(2)}) async-start(), calls=%async_computation | async-start | bytes 524288 | tf_op jit(solution)/shard_map/psum | solution.py:211
  9.4 15.0 %copy-start.17 = (f32[3,128,256]{2,1,0:T(8,128)S(1)}, f32[3,128,256]{2,1,0:T(8,128)}, u32[]{:S(2)}) copy-start(f32[3,128,256]{2,1,0:T(8,128)} %param.45) | copy-start | bytes 1179652
  9.4 15.0 %collective-permute-start = (f32[2,3,128,256]{3,2,1,0:T(8,128)}, f32[2,3,128,256]{3,2,1,0:T(8,128)}, u32[]{:S(2)}, u32[]{:S(2)}) collective-permute-start(f32[2,3,128,256]{3,2,1,0:T(8,128)} %pad_maximum_fusion.22), channel_id=1, source_target_pairs={{4,0},{8,4},{12,8},{16,12},{20,16},{24,20},{28,24},{32,28},{36,32}... | collective-permute-start | bytes 2359304 | tf_op jit(solution)/shard_map/ppermute | solution.py:16
  14.9 0.7 copy-start.20
  55.5 2.0 copy-start.12
  55.5 2.0 copy-start.13
  71.1 2.0 copy-start.23
  71.2 2.0 copy-start.24
  74.3 1.0 copy-start.21
  104.9 21.5 %collective-permute-start.1 = (f32[2,4,2,128,128]{4,3,2,1,0:T(8,128)}, f32[2,4,2,128,128]{4,3,2,1,0:T(8,128)}, u32[]{:S(2)}, u32[]{:S(2)}) collective-permute-start(f32[2,4,2,128,128]{4,3,2,1,0:T(8,128)} %get-tuple-element.1746), channel_id=1, source_target_pairs={{0,1},{1,2},{2,3},{4,5},{5,6},{6,7},{8,9},{9,10},{10,11},{12,13},{... | collective-permute-start | bytes 3145736 | tf_op jit(solution)/shard_map/ppermute | solution.py:22
  135.1 83.7 %collective-permute-start.2 = (f32[2,4,2,128,128]{4,3,2,1,0:T(8,128)}, f32[2,4,2,128,128]{4,3,2,1,0:T(8,128)}, u32[]{:S(2)}, u32[]{:S(2)}) collective-permute-start(f32[2,4,2,128,128]{4,3,2,1,0:T(8,128)} %get-tuple-element.1748), channel_id=1, source_target_pairs={{0,1},{1,2},{2,3},{4,5},{5,6},{6,7},{8,9},{9,10},{10,11},{12,13},{... | collective-permute-start | bytes 3145736 | tf_op jit(solution)/shard_map/ppermute | solution.py:22
  218.9 13.3 %copy-start.40 = (s32[64]{0:T(128)S(1)}, s32[64]{0:T(128)}, u32[]{:S(2)}) copy-start(s32[64]{0:T(128)} %param.51) | copy-start | bytes 772
  227.7 22.7 %collective-permute-start.3 = (f32[2,4,2,128,128]{4,3,2,1,0:T(8,128)}, f32[2,4,2,128,128]{4,3,2,1,0:T(8,128)S(1)}, u32[]{:S(2)}, u32[]{:S(2)}) collective-permute-start(f32[2,4,2,128,128]{4,3,2,1,0:T(8,128)} %get-tuple-element.1750), channel_id=1, source_target_pairs={{0,1},{1,2},{2,3},{4,5},{5,6},{6,7},{8,9},{9,10},{10,11},{12,13},{... | collective-permute-start | bytes 3145736 | tf_op jit(solution)/shard_map/ppermute | solution.py:22
  281.7 81.0 %collective-permute-start.4 = (f32[2,4,2,128,128]{4,3,2,1,0:T(8,128)}, f32[2,4,2,128,128]{4,3,2,1,0:T(8,128)}, u32[]{:S(2)}, u32[]{:S(2)}) collective-permute-start(f32[2,4,2,128,128]{4,3,2,1,0:T(8,128)} %get-tuple-element.1754), channel_id=1, source_target_pairs={{1,0},{2,1},{3,2},{5,4},{6,5},{7,6},{9,8},{10,9},{11,10},{13,12},{... | collective-permute-start | bytes 3145736 | tf_op jit(solution)/shard_map/ppermute | solution.py:22
  371.7 22.1 %collective-permute-start.5 = (f32[2,4,2,128,128]{4,3,2,1,0:T(8,128)}, f32[2,4,2,128,128]{4,3,2,1,0:T(8,128)}, u32[]{:S(2)}, u32[]{:S(2)}) collective-permute-start(f32[2,4,2,128,128]{4,3,2,1,0:T(8,128)} %get-tuple-element.1756), channel_id=1, source_target_pairs={{1,0},{2,1},{3,2},{5,4},{6,5},{7,6},{9,8},{10,9},{11,10},{13,12},{... | collective-permute-start | bytes 3145736 | tf_op jit(solution)/shard_map/ppermute | solution.py:22
  402.7 218.2 %collective-permute-start.6 = (f32[2,4,2,128,128]{4,3,2,1,0:T(8,128)}, f32[2,4,2,128,128]{4,3,2,1,0:T(8,128)S(1)}, u32[]{:S(2)}, u32[]{:S(2)}) collective-permute-start(f32[2,4,2,128,128]{4,3,2,1,0:T(8,128)} %get-tuple-element.1758), channel_id=1, source_target_pairs={{1,0},{2,1},{3,2},{5,4},{6,5},{7,6},{9,8},{10,9},{11,10},{13,12},{... | collective-permute-start | bytes 3145736 | tf_op jit(solution)/shard_map/ppermute | solution.py:22
  673.1 2.0 copy-start.31
  673.1 2.0 copy-start.32
  679.6 1.2 copy-start.5
  680.8 0.7 copy-start.37
  680.8 0.7 copy-start.39
  724.3 197.6 %copy-start.41 = (s32[64]{0:T(128)S(1)}, s32[64]{0:T(128)}, u32[]{:S(2)}) copy-start(s32[64]{0:T(128)} %param.51) | copy-start | bytes 772
  724.3 245.9 %collective-permute-start.7 = (f32[2,3,128,256]{3,2,1,0:T(8,128)}, f32[2,3,128,256]{3,2,1,0:T(8,128)}, u32[]{:S(2)}, u32[]{:S(2)}) collective-permute-start(f32[2,3,128,256]{3,2,1,0:T(8,128)} %slice.537), channel_id=1, source_target_pairs={{252,0},{0,4},{4,8},{8,12},{12,16},{16,20},{20,24},{24,28},{28,32}... | collective-permute-start | bytes 2359304 | tf_op jit(solution)/shard_map/ppermute | solution.py:16
  725.1 246.3 %copy-start.18 = (f32[3,128,256]{2,1,0:T(8,128)S(1)}, f32[3,128,256]{2,1,0:T(8,128)}, u32[]{:S(2)}) copy-start(f32[3,128,256]{2,1,0:T(8,128)} %param.45) | copy-start | bytes 1179652
  725.1 246.3 %copy-start.19 = (f32[3,128,256]{2,1,0:T(8,128)S(1)}, f32[3,128,256]{2,1,0:T(8,128)}, u32[]{:S(2)}) copy-start(f32[3,128,256]{2,1,0:T(8,128)} %param.44) | copy-start | bytes 1179652
  725.1 243.6 %all-reduce.5.cloned.1.call-start = ((), (), s32[]{:S(2)}) async-start(), calls=%async_computation.1 | async-start | bytes 524288 | tf_op jit(solution)/shard_map/psum | solution.py:27
Sparse Core Ops, SparseCore 0:
  725.2 194.9 all-reduce.2
  923.2 45.5 all-reduce.4
where the time goes:
time: 983 us; the launch traced here: 979 us
  waiting for transfers between devices  620 us (63%)
  matrix products  97.2 us (10%)
  loops' own time  97.1 us (10%)
  starting transfers between devices  81.3 us (8%)
  local copies, waits for them, and re-layouts  46 us (5%)
  other arithmetic  22.1 us (2%)
  between operations  15.1 us (2%)
    ppermute x6, waiting for transfers between devices, passed_along(): return lax.ppermute(block, axis, route)  372 us
    psum x1, waiting for transfers between devices, body(): tile_total = lax.psum(probe_grad, 'tile')  195 us
    ppermute x6, starting transfers between devices, passed_along(): return lax.ppermute(block, axis, route)  76.1 us
    psum x1, waiting for transfers between devices, broadcast(): return lax.psum(jnp.where(mine, shard, jnp.zeros_like(shard)), axis)  45.6 us
    another operation x4, loops' own time, body(): lax.cond(depth_index == section_step, run_forward, lambda args_in: args_i...  35.8 us
    another operation x4, loops' own time, body(): lax.cond(depth_index == section_step, run_backward, lambda args_in: args_...  28.6 us
  transfers between devices with their start and end apart: 10, of which 9 were waited for; matrix products, arithmetic and copies ran while one was open for 1% of the time, Pallas kernels for 0%

commit v1 on v0

v1 whole, which is shorter than its diff:
```python
import jax
import jax.numpy as jnp
import numpy as np
from jax import lax
from jax.experimental import pallas as pl
from jax.experimental.pallas import tpu as pltpu
from jax.sharding import PartitionSpec as P

PIX = 128
SLICES = 12
GROUP = 3
PROP_PHASE = 12.0
AMP_EPS = 0.05
OBJ_STEP = 1.0
PROBE_STEP = 4.0


def split_const(matrix):
    high = matrix.astype(np.float32).astype(jnp.bfloat16)
    low = (matrix - high.astype(np.float64)).astype(np.float32).astype(jnp.bfloat16)
    return high, low


def make_constants():
    n = np.arange(PIX)
    dft = np.exp(-2j * np.pi * ((n[:, None] * n[None, :]) % PIX) / PIX) / np.sqrt(PIX)
    freq = ((n + PIX // 2) % PIX - PIX // 2) / PIX
    step = np.conj(dft) @ (np.exp(-1j * PROP_PHASE * freq**2)[:, None] * dft)
    out = []
    for matrix in (step, dft):
        real, imag = matrix.real, matrix.imag
        right = np.block([[real, imag], [-imag, real]])
        left = np.block([[real, -imag], [imag, real]])
        high, low = split_const(right)
        out.append(np.concatenate([high, high, low], axis=0))
        high, low = split_const(left)
        out.append(np.concatenate([high, high, low], axis=1))
    return out


def split(value):
    high = value.astype(jnp.bfloat16)
    low = (value - high.astype(jnp.float32)).astype(jnp.bfloat16)
    return high, low


def sandwich(field, right, left):
    wide = jnp.concatenate(
        [jnp.concatenate([field[0][m], field[1][m]], axis=1) for m in range(2)], axis=0
    )
    high, low = split(wide)
    middle = jnp.dot(
        jnp.concatenate([high, low, high], axis=1), right, preferred_element_type=jnp.float32
    )
    tall = jnp.concatenate(
        [
            jnp.concatenate([middle[:PIX, c * PIX : (c + 1) * PIX], middle[PIX:, c * PIX : (c + 1) * PIX]], axis=1)
            for c in range(2)
        ],
        axis=0,
    )
    high, low = split(tall)
    done = jnp.dot(
        left, jnp.concatenate([high, low, high], axis=0), preferred_element_type=jnp.float32
    )
    return [[done[c * PIX : (c + 1) * PIX, m * PIX : (m + 1) * PIX] for m in range(2)] for c in range(2)]


def times(patch_real, patch_imag, field):
    real = [field[0][m] * patch_real - field[1][m] * patch_imag for m in range(2)]
    imag = [field[0][m] * patch_imag + field[1][m] * patch_real for m in range(2)]
    return [real, imag]


def chain_kernel(
    live_ref, patch_ref, probe_real, probe_imag, measured_ref,
    step_right, step_left, dft_right, dft_left,
    piece_ref, probe_grad, waves,
):
    def load(ref, k):
        return [[ref[k, c, m] for m in range(2)] for c in range(2)]

    def store(ref, k, field):
        for c in range(2):
            for m in range(2):
                ref[k, c, m] = field[c][m]

    store(waves, 0, [[probe_real[m] for m in range(2)], [probe_imag[m] for m in range(2)]])

    def forward(k, carry):
        chi = times(patch_ref[k, 0], patch_ref[k, 1], load(waves, k))
        store(waves, k + 1, sandwich(chi, step_right[...], step_left[...]))
        return carry

    lax.fori_loop(0, SLICES - 1, forward, 0)
    last = SLICES - 1
    exit_wave = times(patch_ref[last, 0], patch_ref[last, 1], load(waves, last))
    far = sandwich(exit_wave, dft_right[...], dft_left[...])
    intensity = sum(far[c][m] * far[c][m] for c in range(2) for m in range(2))
    factor = (1.0 - measured_ref[...] * lax.rsqrt(intensity + AMP_EPS)) * live_ref[0]
    bent = [[far[0][m] * factor for m in range(2)], [-far[1][m] * factor for m in range(2)]]
    grad = sandwich(bent, dft_right[...], dft_left[...])

    def collect(k, grad):
        wave = load(waves, k)
        piece_ref[k, 0] = sum(wave[0][m] * grad[0][m] - wave[1][m] * grad[1][m] for m in range(2))
        piece_ref[k, 1] = -sum(wave[0][m] * grad[1][m] + wave[1][m] * grad[0][m] for m in range(2))
        return times(patch_ref[k, 0], patch_ref[k, 1], grad)

    store(waves, SLICES, grad)

    def backward(i, carry):
        k = last - i
        bent = collect(k, load(waves, SLICES))
        store(waves, SLICES, sandwich(bent, step_right[...], step_left[...]))
        return carry

    lax.fori_loop(0, SLICES - 1, backward, 0)
    entry = collect(0, load(waves, SLICES))
    for m in range(2):
        probe_grad[0, m] = entry[0][m]
        probe_grad[1, m] = -entry[1][m]


def run_chain(live, patches, probe_real, probe_imag, measured):
    vmem = pl.BlockSpec(memory_space=pltpu.VMEM)
    smem = pl.BlockSpec(memory_space=pltpu.SMEM)
    return pl.pallas_call(
        chain_kernel,
        out_shape=(
            jax.ShapeDtypeStruct((SLICES, 2, PIX, PIX), jnp.float32),
            jax.ShapeDtypeStruct((2, 2, PIX, PIX), jnp.float32),
        ),
        in_specs=[smem] + [vmem] * 8,
        out_specs=(vmem, vmem),
        scratch_shapes=[pltpu.VMEM((SLICES + 1, 2, 2, PIX, PIX), jnp.float32)],
        compiler_params=pltpu.CompilerParams(vmem_limit_bytes=40 * 1024 * 1024),
    )(live, patches, probe_real, probe_imag, measured, *[jnp.asarray(c) for c in make_constants()])


def shifted(block, axis, distance):
    count = lax.axis_size(axis)
    return lax.ppermute(block, axis, [((i - distance) % count, i) for i in range(count)])


def body(
    object_real, object_imag, probe_real, probe_imag, measured, row_offset, col_offset, counts
):
    slices_dev, rows_dev, _ = object_real.shape
    slot_count = row_offset.shape[0]
    depth_index = lax.axis_index("depth")
    depth_count = lax.axis_size("depth")
    objects = jnp.stack([object_real, object_imag], axis=1)
    extended = jnp.concatenate([objects, shifted(objects, "tile", -1)], axis=2)
    patches = jnp.stack(
        [
            lax.dynamic_slice(extended, (0, 0, row_offset[s], col_offset[s]), (slices_dev, 2, PIX, PIX))
            for s in range(slot_count)
        ]
    )
    mine = lax.all_to_all(patches, "depth", 0, 0, tiled=True).reshape(SLICES, 2, PIX, PIX)
    own_count = lax.dynamic_index_in_dim(counts, lax.axis_index("tile"), 0, keepdims=False)
    live = (depth_index < own_count).astype(jnp.float32).reshape(1)
    own_measured = lax.dynamic_index_in_dim(measured, depth_index, 0, keepdims=False)
    pieces, probe_grad = run_chain(live, mine, probe_real, probe_imag, own_measured)
    back = lax.all_to_all(
        pieces.reshape(depth_count, slices_dev, 2, PIX, PIX), "depth", 0, 0, tiled=True
    )
    total = jnp.zeros_like(extended)
    for s in range(slot_count):
        start = (0, 0, row_offset[s], col_offset[s])
        block = lax.dynamic_slice(total, start, (slices_dev, 2, PIX, PIX))
        total = lax.dynamic_update_slice(total, block + back[s], start)
    object_grad = total[:, :, :rows_dev] + shifted(total[:, :, rows_dev:], "tile", 1)
    rows = PIX // depth_count
    grad_mine = lax.psum_scatter(probe_grad, "depth", scatter_dimension=2, tiled=True)
    grad_mine = lax.psum(grad_mine, "tile")
    real_mine = lax.dynamic_slice_in_dim(probe_real, depth_index * rows, rows, 1)
    imag_mine = lax.dynamic_slice_in_dim(probe_imag, depth_index * rows, rows, 1)
    live_total = jnp.sum(counts).astype(jnp.float32)
    return (
        object_real - OBJ_STEP * object_grad[:, 0],
        object_imag - OBJ_STEP * object_grad[:, 1],
        real_mine - PROBE_STEP * grad_mine[0] / live_total,
        imag_mine - PROBE_STEP * grad_mine[1] / live_total,
    )


def solution(mesh):
    placed = (
        P("depth", "tile", None),
        P("depth", "tile", None),
        P(),
        P(),
        P("tile", None, None),
        P("tile"),
        P("tile"),
        P(),
    )
    return jax.shard_map(
        body,
        mesh=mesh,
        in_specs=placed,
        out_specs=(
            P("depth", "tile", None),
            P("depth", "tile", None),
            P(None, "depth", None),
            P(None, "depth", None),
        ),
        check_vma=False,
    )
```

time: 983 us -> 327 us (0.33)
  waiting for transfers between devices: 620 us -> 215 us
  matrix products: 97.2 us -> 0 us
  loops' own time: 97.1 us -> 0 us
  starting transfers between devices: 81.3 us -> 9.82 us
  local copies, waits for them, and re-layouts: 46 us -> 24.2 us
  blocking collectives: 0 us -> 17.4 us
  Pallas kernels: 0 us -> 17.2 us
  between operations: 15.1 us -> 30.9 us
  other arithmetic: 22.1 us -> 9.79 us
    ppermute x8 -> x2, waiting for transfers between devices: 380 us -> 0.01 us  [shifted(): lax.ppermute(block, axis, [((i - distance) % count, i) for i in range(cou...]
    dot_general x96 -> x0, matrix products: 97.2 us -> none  [the longest x12 14.7 us: right_apply(): jnp.einsum('...nm,ml->...nl', field_imag, dft_imag, precision=PRECISE)]
    another operation x13 -> x0, loops' own time: 97.1 us -> none  [the longest x4 35.8 us: body(): lax.cond(depth_index == section_step, run_forward, lambda args_in: args_i...]
    ppermute x8 -> x2, starting transfers between devices: 81.3 us -> 5.34 us  [shifted(): lax.ppermute(block, axis, [((i - distance) % count, i) for i in range(cou...]
    psum x2 -> x1, waiting for transfers between devices: 241 us -> 170 us  [body(): grad_mine = lax.psum(grad_mine, 'tile')]
    reduce_scatter x0 -> x1, waiting for transfers between devices: none -> 30.2 us  [body(): lax.psum_scatter(probe_grad, 'depth', scatter_dimension=2, tiled=True)]
    all_to_all x0 -> x1, blocking collectives: none -> 17.4 us  [body(): lax.all_to_all(pieces.reshape(depth_count, slices_dev, 2, PIX, PIX), 'dep...]
    pallas_call x0 -> x1, Pallas kernels: none -> 17.2 us  [run_chain(): pl.pallas_call(chain_kernel, out_shape=(jax.ShapeDtypeStruct((SLICES, 2,...]
  transfers between devices with their start and end apart: 10 -> 5, of which waited for: 9 -> 3; matrix products, arithmetic and copies ran while one was open for 1% -> 1% of each run, Pallas kernels for 0% -> 0%
where the time goes in v1:
time: 327 us; the launch traced here: 324 us
  waiting for transfers between devices  215 us (66%)
  between operations  30.9 us (9%)
  local copies, waits for them, and re-layouts  24.2 us (7%)
  blocking collectives  17.4 us (5%)
  Pallas kernels  17.2 us (5%)
  starting transfers between devices  9.82 us (3%)
  other arithmetic  9.79 us (3%)
    psum x1, waiting for transfers between devices, body(): grad_mine = lax.psum(grad_mine, 'tile')  170 us
    reduce_scatter x1, waiting for transfers between devices, body(): lax.psum_scatter(probe_grad, 'depth', scatter_dimension=2, tiled=True)  30.2 us
    dynamic_update_slice x4, local copies, waits for them, and re-layouts, body(): total = lax.dynamic_update_slice(total, block + back[s], start)  18.8 us
    all_to_all x1, blocking collectives, body(): lax.all_to_all(pieces.reshape(depth_count, slices_dev, 2, PIX, PIX), 'dep...  17.4 us
    pallas_call x1, Pallas kernels, run_chain(): pl.pallas_call(chain_kernel, out_shape=(jax.ShapeDtypeStruct((SLICES, 2,...  17.2 us
    all_to_all x1, waiting for transfers between devices, body(): lax.all_to_all(patches, 'depth', 0, 0, tiled=True)  14.9 us
  transfers between devices with their start and end apart: 5, of which 3 were waited for; matrix products, arithmetic and copies ran while one was open for 1% of the time, Pallas kernels for 0%

profile of v1, /device:TPU:8, one launch (start us, length us, event | category | flops | bytes accessed | tf_op | source)
XLA Modules:
  0.0 324.0 jit_solution(14687238534509631464)
XLA Ops:
  7.2 1.2 pad_maximum_fusion.2
  8.5 5.3 %collective-permute-start = (f32[3,2,128,256]{3,2,1,0:T(8,128)S(1)}, f32[3,2,128,256]{3,2,1,0:T(8,128)S(1)}, u32[]{:S(2)}, u32[]{:S(2)}) collective-permute-start(f32[3,2,128,256]{3,2,1,0:T(8,128)S(1)} %pad_maximum_fusion.2), channel_id=1, source_target_pairs={{4,0},{8,4},{12,8},{16,12},{20,16},{24,20},{28,24},{32,28},{36,32}... | collective-permute-start | bytes 2359304 | tf_op jit(solution)/shard_map/ppermute | solution.py:143
  13.7 0.6 fusion.12
  19.5 0.7 fusion.11
  30.3 0.2 pad_maximum_fusion
  30.5 0.5 dynamic-slice_bitcast_fusion.3
  31.0 1.3 pad_maximum_fusion.1
  32.3 4.4 %all-to-all-start = ((f32[4,3,2,128,128]{4,3,2,1,0:T(8,128)}), f32[4,3,2,128,128]{4,3,2,1,0:T(8,128)S(1)}, u32[]{:S(2)}, u32[]{:S(2)}) async-start(f32[4,3,2,128,128]{4,3,2,1,0:T(8,128)} %pad_maximum_fusion.1), calls=%async_computation | async-start | bytes 3145728 | tf_op jit(solution)/shard_map/all_to_all | solution.py:161
  36.8 0.6 dynamic_slice.35
  38.0 14.9 %all-to-all-done = f32[4,3,2,128,128]{4,3,2,1,0:T(8,128)S(1)} async-done(((f32[4,3,2,128,128]{4,3,2,1,0:T(8,128)}), f32[4,3,2,128,128]{4,3,2,1,0:T(8,128)S(1)}, u32[]{:S(2)}, u32[]{:S(2)}) %all-to-all-start) | async-done | bytes 1572896 | tf_op jit(solution)/shard_map/all_to_all | solution.py:161
  53.0 0.9 copy-done.5
  53.9 0.9 copy-done.6
  54.8 17.2 %shard_map.147 = (f32[12,2,128,128]{3,2,1,0:T(8,128)S(1)}, f32[2,2,128,128]{3,2,1,0:T(8,128)}) custom-call(f32[1]{0:T(128)} %bitcast.1.live_ref, f32[12,2,128,128]{3,2,1,0:T(8,128)S(1)} %bitcast.54, f32[2,128,128]{2,1,0:T(8,128)S(1)} %copy-done.5, f32[2,128,128]{2,1,0:T(8,128)S(1)} %copy-done.6, f32[128,128]{1,0:T(8,128)S(1)} %dynamic-slice_bitcast_fusion.4.measured_ref, ...), custom_call_target="tpu_custom_call" | custom-call | tf_op jit(solution)/shard_map/pallas_call | solution.py:128
  72.0 0.1 copy.17
  72.1 17.4 %all_to_all.10 = f32[4,3,2,128,128]{4,3,1,2,0:T(8,128)S(1)} all-to-all(f32[4,3,2,128,128]{4,3,1,2,0:T(8,128)S(1)} %copy.17), channel_id=1, replica_groups=mesh['tile'=64,'depth'=4] {'depth'}, dimensions={0} | all-to-all | bytes 3145728 | tf_op jit(solution)/shard_map/all_to_all | solution.py:166
  89.6 0.8 slice_bitcast_fusion.5
  90.3 0.1 broadcast_in_dim.3
  90.5 4.8 %dynamic_update_slice.12 = f32[3,2,256,256]{3,2,0,1:T(8,128)S(1)} dynamic-update-slice(f32[3,2,256,256]{3,2,0,1:T(8,128)S(1)} %broadcast_in_dim.3, f32[3,2,128,128]{3,2,0,1:T(8,128)} %slice_bitcast_fusion.5, s32[]{:T(128)} %constant.13.clone.1, s32[]{:T(128)} %constant.13.clone.1, s32[]{:T(128)S(6)} %select_n.27, s32[]{:T(128)S(6)} %select_n.52) | dynamic-update-slice | bytes 786436 | tf_op jit(solution)/shard_map/dynamic_update_slice | solution.py:173
  95.3 0.9 fusion.4
  96.3 4.8 %dynamic_update_slice.13 = f32[3,2,256,256]{3,2,0,1:T(8,128)S(1)} dynamic-update-slice(f32[3,2,256,256]{3,2,0,1:T(8,128)S(1)} %dynamic_update_slice.12, f32[3,2,128,128]{3,2,0,1:T(8,128)} %fusion.4, s32[]{:T(128)} %constant.13.clone.1, s32[]{:T(128)} %constant.13.clone.1, s32[]{:T(128)S(6)} %select_n.53, s32[]{:T(128)S(6)} %select_n.54) | dynamic-update-slice | bytes 786436 | tf_op jit(solution)/shard_map/dynamic_update_slice | solution.py:173
  101.0 0.9 fusion.3
  102.0 4.6 %dynamic_update_slice.14 = f32[3,2,256,256]{3,2,0,1:T(8,128)S(1)} dynamic-update-slice(f32[3,2,256,256]{3,2,0,1:T(8,128)S(1)} %dynamic_update_slice.13, f32[3,2,128,128]{3,2,0,1:T(8,128)} %fusion.3, s32[]{:T(128)} %constant.13.clone.1, s32[]{:T(128)} %constant.13.clone.1, s32[]{:T(128)S(6)} %select_n.55, s32[]{:T(128)S(6)} %select_n.56) | dynamic-update-slice | bytes 786436 | tf_op jit(solution)/shard_map/dynamic_update_slice | solution.py:173
  106.6 0.9 fusion.2
  107.5 4.6 %dynamic_update_slice.15 = f32[3,2,256,256]{3,2,0,1:T(8,128)S(1)} dynamic-update-slice(f32[3,2,256,256]{3,2,0,1:T(8,128)S(1)} %dynamic_update_slice.14, f32[3,2,128,128]{3,2,0,1:T(8,128)} %fusion.2, s32[]{:T(128)} %constant.13.clone.1, s32[]{:T(128)} %constant.13.clone.1, s32[]{:T(128)S(6)} %select_n.57, s32[]{:T(128)S(6)} %select_n.58) | dynamic-update-slice | bytes 786436 | tf_op jit(solution)/shard_map/dynamic_update_slice | solution.py:173
  112.1 0.1 slice.85
  112.2 0.1 collective-permute-start.1
  112.4 30.2 %reduce-scatter.2.cloned.1.call-done = f32[2,2,32,128]{3,2,1,0:T(8,128)} async-done(((f32[2,2,128,128]{3,2,1,0:T(8,128)}), f32[2,2,32,128]{3,2,1,0:T(8,128)}) %reduce-scatter.2.cloned.1.call-update) | async-done | bytes 65552 | tf_op jit(solution)/shard_map/reduce_scatter | solution.py:176
  142.6 0.6 reduce_sum.9
  143.9 169.6 %all-reduce.2.cloned.1.call-done = f32[2,2,32,128]{3,2,1,0:T(8,128)} async-done(((f32[2,2,32,128]{3,2,1,0:T(8,128)}), f32[2,2,32,128]{3,2,1,0:T(8,128)}) %all-reduce.2.cloned.1.call-update) | async-done | bytes 65552 | tf_op jit(solution)/shard_map/psum | solution.py:177
  313.5 1.4 fusion.7
  314.9 1.2 slice_add_fusion
  316.2 1.0 fusion
  (33 shorter events, 0.2 us)
Async XLA Ops:
  7.2 30.8 %copy-start = (f32[4,128,128]{2,1,0:T(8,128)S(1)}, f32[4,128,128]{2,1,0:T(8,128)}, u32[]{:S(2)}) copy-start(f32[4,128,128]{2,1,0:T(8,128)} %param.16) | copy-start | bytes 786436
  7.2 23.1 %copy-start.7 = (f32[3,128,256]{2,1,0:T(8,128)S(1)}, f32[3,128,256]{2,1,0:T(8,128)}, u32[]{:S(2)}) copy-start(f32[3,128,256]{2,1,0:T(8,128)} %param.13) | copy-start | bytes 1179652
  7.2 23.1 %copy-start.9 = (f32[3,128,256]{2,1,0:T(8,128)S(1)}, f32[3,128,256]{2,1,0:T(8,128)}, u32[]{:S(2)}) copy-start(f32[3,128,256]{2,1,0:T(8,128)} %param.12) | copy-start | bytes 1179652
  7.2 6.5 %copy-start.11 = (s32[4]{0:T(128)S(1)}, s32[4]{0:T(128)}, u32[]{:S(2)}) copy-start(s32[4]{0:T(128)} %param.17) | copy-start | bytes 52
  7.2 12.3 %copy-start.12 = (s32[4]{0:T(128)S(1)}, s32[4]{0:T(128)}, u32[]{:S(2)}) copy-start(s32[4]{0:T(128)} %param.18) | copy-start | bytes 52
  8.5 21.8 %collective-permute-start = (f32[3,2,128,256]{3,2,1,0:T(8,128)S(1)}, f32[3,2,128,256]{3,2,1,0:T(8,128)S(1)}, u32[]{:S(2)}, u32[]{:S(2)}) collective-permute-start(f32[3,2,128,256]{3,2,1,0:T(8,128)S(1)} %pad_maximum_fusion.2), channel_id=1, source_target_pairs={{4,0},{8,4},{12,8},{16,12},{20,16},{24,20},{28,24},{32,28},{36,32}... | collective-permute-start | bytes 2359304 | tf_op jit(solution)/shard_map/ppermute | solution.py:143
  32.3 4.5 %copy-start.13 = (s32[64]{0:T(128)S(1)}, s32[64]{0:T(128)}, u32[]{:S(2)}) copy-start(s32[64]{0:T(128)} %param.19) | copy-start | bytes 772
  32.3 20.7 %copy-start.1 = (bf16[256,768]{1,0:T(8,128)(2,1)S(1)}, bf16[256,768]{1,0:T(8,128)(2,1)}, u32[]{:S(2)}) copy-start(bf16[256,768]{1,0:T(8,128)(2,1)} %constant.42.clone.dft_left) | copy-start | bytes 1179652
  32.3 20.7 %copy-start.2 = (bf16[768,256]{1,0:T(8,128)(2,1)S(1)}, bf16[768,256]{1,0:T(8,128)(2,1)}, u32[]{:S(2)}) copy-start(bf16[768,256]{1,0:T(8,128)(2,1)} %constant.41.clone.dft_right) | copy-start | bytes 1179652
  32.3 20.7 %copy-start.3 = (bf16[256,768]{1,0:T(8,128)(2,1)S(1)}, bf16[256,768]{1,0:T(8,128)(2,1)}, u32[]{:S(2)}) copy-start(bf16[256,768]{1,0:T(8,128)(2,1)} %constant.40.clone.step_left) | copy-start | bytes 1179652
  32.3 20.7 %copy-start.4 = (bf16[768,256]{1,0:T(8,128)(2,1)S(1)}, bf16[768,256]{1,0:T(8,128)(2,1)}, u32[]{:S(2)}) copy-start(bf16[768,256]{1,0:T(8,128)(2,1)} %constant.39.clone.step_right) | copy-start | bytes 1179652
  32.3 20.6 %all-to-all-start = ((f32[4,3,2,128,128]{4,3,2,1,0:T(8,128)}), f32[4,3,2,128,128]{4,3,2,1,0:T(8,128)S(1)}, u32[]{:S(2)}, u32[]{:S(2)}) async-start(f32[4,3,2,128,128]{4,3,2,1,0:T(8,128)} %pad_maximum_fusion.1), calls=%async_computation | async-start | bytes 3145728 | tf_op jit(solution)/shard_map/all_to_all | solution.py:161
  36.7 105.9 %reduce-scatter.2.cloned.1.call-start = ((), (), s32[]{:S(2)}) async-start(), calls=%async_computation.3 | async-start | bytes 327680 | tf_op jit(solution)/shard_map/reduce_scatter | solution.py:176
  53.0 0.9 copy-start.5
  53.9 0.9 copy-start.6
  112.2 204.0 %copy-start.8 = (f32[3,128,256]{2,1,0:T(8,128)S(1)}, f32[3,128,256]{2,1,0:T(8,128)}, u32[]{:S(2)}) copy-start(f32[3,128,256]{2,1,0:T(8,128)} %param.13) | copy-start | bytes 1179652
  112.2 204.0 %copy-start.10 = (f32[3,128,256]{2,1,0:T(8,128)S(1)}, f32[3,128,256]{2,1,0:T(8,128)}, u32[]{:S(2)}) copy-start(f32[3,128,256]{2,1,0:T(8,128)} %param.12) | copy-start | bytes 1179652
  112.2 202.7 %collective-permute-start.1 = (f32[3,2,128,256]{3,2,0,1:T(8,128)S(1)}, f32[3,2,128,256]{3,2,0,1:T(8,128)}, u32[]{:S(2)}, u32[]{:S(2)}) collective-permute-start(f32[3,2,128,256]{3,2,0,1:T(8,128)S(1)} %slice.85), channel_id=1, source_target_pairs={{252,0},{0,4},{4,8},{8,12},{12,16},{16,20},{20,24},{24,28},{28,32}... | collective-permute-start | bytes 2359304 | tf_op jit(solution)/shard_map/ppermute | solution.py:143
  112.4 201.1 %all-reduce.2.cloned.1.call-start = ((), (), s32[]{:S(2)}) async-start(), calls=%async_computation.4 | async-start | bytes 131072 | tf_op jit(solution)/shard_map/psum | solution.py:177
Sparse Core Ops, SparseCore 0:
  112.5 30.0 reduce-scatter.1
  146.5 166.9 all-reduce.1

commit v2 on v1

v2 whole, which is shorter than its diff:
```python
import functools

import jax
import jax.numpy as jnp
import numpy as np
from jax import lax
from jax.experimental import pallas as pl
from jax.experimental.pallas import tpu as pltpu
from jax.sharding import PartitionSpec as P

PIX = 128
SLICES = 12
GROUP = 3
RING = 16
PROP_PHASE = 12.0
AMP_EPS = 0.05
OBJ_STEP = 1.0
PROBE_STEP = 4.0


def split_const(matrix):
    high = matrix.astype(np.float32).astype(jnp.bfloat16)
    low = (matrix - high.astype(np.float64)).astype(np.float32).astype(jnp.bfloat16)
    return high, low


def make_constants():
    n = np.arange(PIX)
    dft = np.exp(-2j * np.pi * ((n[:, None] * n[None, :]) % PIX) / PIX) / np.sqrt(PIX)
    freq = ((n + PIX // 2) % PIX - PIX // 2) / PIX
    step = np.conj(dft) @ (np.exp(-1j * PROP_PHASE * freq**2)[:, None] * dft)
    out = []
    for matrix in (step, dft):
        real, imag = matrix.real, matrix.imag
        right = np.block([[real, imag], [-imag, real]])
        left = np.block([[real, -imag], [imag, real]])
        high, low = split_const(right)
        out.append(np.concatenate([high, high, low], axis=0))
        high, low = split_const(left)
        out.append(np.concatenate([high, high, low], axis=1))
    return out


def split(value):
    high = value.astype(jnp.bfloat16)
    low = (value - high.astype(jnp.float32)).astype(jnp.bfloat16)
    return high, low


def sandwich(field, right, left):
    wide = jnp.concatenate(
        [jnp.concatenate([field[0][m], field[1][m]], axis=1) for m in range(2)], axis=0
    )
    high, low = split(wide)
    middle = jnp.dot(
        jnp.concatenate([high, low, high], axis=1), right, preferred_element_type=jnp.float32
    )
    tall = jnp.concatenate(
        [
            jnp.concatenate([middle[:PIX, c * PIX : (c + 1) * PIX], middle[PIX:, c * PIX : (c + 1) * PIX]], axis=1)
            for c in range(2)
        ],
        axis=0,
    )
    high, low = split(tall)
    done = jnp.dot(
        left, jnp.concatenate([high, low, high], axis=0), preferred_element_type=jnp.float32
    )
    return [[done[c * PIX : (c + 1) * PIX, m * PIX : (m + 1) * PIX] for m in range(2)] for c in range(2)]


def times(patch_real, patch_imag, field):
    real = [field[0][m] * patch_real - field[1][m] * patch_imag for m in range(2)]
    imag = [field[0][m] * patch_imag + field[1][m] * patch_real for m in range(2)]
    return [real, imag]


MESH = pl.DeviceIdType.MESH


def turned(block, rows, cols):
    return pltpu.roll(pltpu.roll(block, rows, 0), cols, 1)


def kernel(
    n_tile, n_depth, ring,
    row_ref, col_ref, count_ref, obj_real, obj_imag, probe_real, probe_imag, measured_ref,
    step_right, step_left, dft_right, dft_left,
    new_real, new_imag, new_probe_real, new_probe_imag,
    head, stage, patch_ref, waves, piece_stage, grads, own_sum, next_sum, next_recv,
    parts, parts_recv, line, line_recv, cross_recv, final,
    head_send_sem, head_recv_sem, patch_send_sem, patch_recv_sem, piece_send_sem, grad_recv_sem,
    next_send_sem, next_recv_sem, part_send_sem, part_recv_sem, line_send_sem, line_recv_sem,
    cross_send_sem, cross_recv_sem, final_send_sem, final_recv_sem,
):
    objects = (obj_real, obj_imag)
    tile = lax.axis_index("tile")
    depth = lax.axis_index("depth")
    after, before = lax.rem(tile + 1, n_tile), lax.rem(tile + n_tile - 1, n_tile)
    n_line = n_tile // ring
    spot, row_of = lax.rem(tile, ring), tile // ring
    ring_base = row_of * ring

    def send(src, dst, send_sem, recv_sem, to_tile, to_depth):
        return pltpu.make_async_remote_copy(
            src_ref=src, dst_ref=dst, send_sem=send_sem, recv_sem=recv_sem,
            device_id=(to_tile, to_depth), device_id_type=MESH,
        )

    def ring_peer(i):
        return lax.rem(spot + i, ring)

    def line_peer(i):
        return lax.rem(row_of + i, n_line)

    def depth_peer(i):
        return lax.rem(depth + i, n_depth)

    barrier = pltpu.get_barrier_semaphore()

    def greet(to_tile, to_depth):
        pl.semaphore_signal(barrier, inc=1, device_id=(to_tile, to_depth), device_id_type=MESH)

    greet(after, depth)
    greet(before, depth)
    lax.fori_loop(1, n_depth, lambda i, c: (greet(tile, depth_peer(i)), c)[1], 0)
    lax.fori_loop(1, ring, lambda i, c: (greet(ring_base + ring_peer(i), depth), c)[1], 0)
    lax.fori_loop(1, n_line, lambda i, c: (greet(line_peer(i) * ring + spot, depth), c)[1], 0)
    pl.semaphore_wait(barrier, 2 + n_depth - 1 + ring - 1 + n_line - 1)

    def head_copy(j, c):
        return send(objects[c].at[j], head.at[j, c], head_send_sem.at[j, c], head_recv_sem.at[j, c], before, depth)

    for j in range(GROUP):
        for c in range(2):
            head_copy(j, c).start()

    row_iota = lax.broadcasted_iota(jnp.int32, (PIX, PIX), 0)
    col_iota = lax.broadcasted_iota(jnp.int32, (PIX, PIX), 1)

    def patch_copy(j, to_depth):
        k = depth * GROUP + j
        return send(
            stage.at[j, to_depth], patch_ref.at[k],
            patch_send_sem.at[j, to_depth], patch_recv_sem.at[k], tile, to_depth,
        )

    def cut(j, i):
        slot = depth_peer(i)
        row, col = row_ref[slot], col_ref[slot]
        own_row, left_col = row_iota >= row, col_iota >= col
        out = []
        for c in range(2):
            upper = jnp.where(left_col, objects[c][j, :, :PIX], objects[c][j, :, PIX:])
            lower = jnp.where(left_col, head[j, c, :, :PIX], head[j, c, :, PIX:])
            block = jnp.where(own_row, upper, lower)
            out.append(turned(block, lax.rem(PIX - row, PIX), lax.rem(PIX - col + PIX, PIX)))
        return slot, out

    def cut_slice(j, carry):
        for c in range(2):
            send(objects[0].at[j], head.at[j, c], head_send_sem.at[j, c], head_recv_sem.at[j, c], before, depth).wait_recv()

        def cut_slot(i, carry):
            slot, out = cut(j, i)
            for c in range(2):
                stage[j, slot, c] = out[c]
            patch_copy(j, slot).start()
            return carry

        lax.fori_loop(1, n_depth, cut_slot, 0)
        _, out = cut(j, 0)
        for c in range(2):
            patch_ref[depth * GROUP + j, c] = out[c]
        return carry

    lax.fori_loop(0, GROUP, cut_slice, 0)

    def load(ref, k):
        return [[ref[k, c, m] for m in range(2)] for c in range(2)]

    def store(ref, k, field):
        for c in range(2):
            for m in range(2):
                ref[k, c, m] = field[c][m]

    def patch_ready(k):
        @pl.when(k // GROUP != depth)
        def _():
            send(stage.at[0, 0], patch_ref.at[k], patch_send_sem.at[0, 0], patch_recv_sem.at[k], tile, depth).wait_recv()

    store(waves, 0, [[probe_real[m] for m in range(2)], [probe_imag[m] for m in range(2)]])

    def forward(k, carry):
        patch_ready(k)
        chi = times(patch_ref[k, 0], patch_ref[k, 1], load(waves, k))
        store(waves, k + 1, sandwich(chi, step_right[...], step_left[...]))
        return carry

    last = SLICES - 1
    lax.fori_loop(0, last, forward, 0)
    patch_ready(last)
    exit_wave = times(patch_ref[last, 0], patch_ref[last, 1], load(waves, last))
    far = sandwich(exit_wave, dft_right[...], dft_left[...])
    intensity = sum(far[c][m] * far[c][m] for c in range(2) for m in range(2))
    live = jnp.where(depth < count_ref[tile], 1.0, 0.0)
    factor = (1.0 - measured_ref[depth] * lax.rsqrt(intensity + AMP_EPS)) * live
    bent = [[far[0][m] * factor for m in range(2)], [-far[1][m] * factor for m in range(2)]]
    store(waves, SLICES, sandwich(bent, dft_right[...], dft_left[...]))

    own_turn = (row_ref[depth], col_ref[depth])

    def collect(k, grad):
        wave = load(waves, k)
        real = sum(wave[0][m] * grad[0][m] - wave[1][m] * grad[1][m] for m in range(2))
        imag = -sum(wave[0][m] * grad[1][m] + wave[1][m] * grad[0][m] for m in range(2))
        row, col = own_turn
        piece_stage[k, 0] = turned(real, row, lax.rem(col, PIX))
        piece_stage[k, 1] = turned(imag, row, lax.rem(col, PIX))
        return times(patch_ref[k, 0], patch_ref[k, 1], grad)

    def piece_copy(k):
        return send(
            piece_stage.at[k], grads.at[lax.rem(k, GROUP), depth],
            piece_send_sem.at[k], grad_recv_sem.at[lax.rem(k, GROUP), depth], tile, k // GROUP,
        )

    def deliver(k):
        @pl.when(k // GROUP != depth)
        def _():
            piece_copy(k).start()

        @pl.when(k // GROUP == depth)
        def _():
            grads[lax.rem(k, GROUP), depth] = piece_stage[k]

    def backward(i, carry):
        k = last - i
        bent = collect(k, load(waves, SLICES))
        store(waves, SLICES, sandwich(bent, step_right[...], step_left[...]))
        deliver(k)
        return carry

    lax.fori_loop(0, last, backward, 0)
    entry = collect(0, load(waves, SLICES))
    deliver(0)

    quarter = PIX // n_depth
    height = 4 * quarter // ring
    for c in range(2):
        for m in range(2):
            value = entry[c][m] if c == 0 else -entry[c][m]
            for d in range(n_depth):
                for i in range(0, quarter, 8):
                    flat = (c * 2 + m) * quarter + i
                    parts[flat // height, d, flat % height : flat % height + 8] = value[
                        d * quarter + i : d * quarter + i + 8
                    ]

    def part_copy(i):
        to = ring_peer(i)
        return send(
            parts.at[to], parts_recv.at[spot], part_send_sem.at[to], part_recv_sem.at[spot],
            ring_base + to, depth,
        )

    def line_copy(i):
        to = line_peer(i)
        return send(
            line, line_recv.at[row_of], line_send_sem.at[to], line_recv_sem.at[row_of],
            to * ring + spot, depth,
        )

    def cross_copy(i):
        to = depth_peer(i)
        return send(
            line_recv.at[n_line, to], cross_recv.at[depth], cross_send_sem.at[to], cross_recv_sem.at[depth],
            tile, to,
        )

    def final_copy(i):
        to = ring_peer(i)
        return send(
            cross_recv.at[n_depth], final.at[spot], final_send_sem.at[to], final_recv_sem.at[spot],
            ring_base + to, depth,
        )

    def start_all(copy, count):
        lax.fori_loop(1, count, lambda i, c: (copy(i).start(), c)[1], 0)

    def wait_sent(copy, count):
        lax.fori_loop(1, count, lambda i, c: (copy(i).wait_send(), c)[1], 0)

    def wait_got(buffer, send_sem, recv_sem, peer, count):
        def one(i, carry):
            frm = peer(i)
            send(buffer.at[frm], buffer.at[frm], send_sem.at[frm], recv_sem.at[frm], tile, depth).wait_recv()
            return carry

        lax.fori_loop(1, count, one, 0)

    parts_recv[spot] = parts[spot]
    start_all(part_copy, ring)

    def next_copy(j):
        return send(next_sum.at[j], next_recv.at[j], next_send_sem.at[j], next_recv_sem.at[j], after, depth)

    def gather_slice(j):
        def arrived(i, carry):
            frm = depth_peer(i)
            send(grads.at[j, frm], grads.at[j, frm], grad_recv_sem.at[j, frm], grad_recv_sem.at[j, frm], tile, depth).wait_recv()
            return carry

        lax.fori_loop(1, n_depth, arrived, 0)
        for c in range(2):
            sums = [0.0] * 4
            for slot in range(n_depth):
                own_row, left_col = row_iota >= row_ref[slot], col_iota >= col_ref[slot]
                block = grads[j, slot, c]
                upper = jnp.where(own_row, block, 0.0)
                lower = block - upper
                upper_left = jnp.where(left_col, upper, 0.0)
                lower_left = jnp.where(left_col, lower, 0.0)
                terms = (upper_left, upper - upper_left, lower_left, lower - lower_left)
                sums = [a + b for a, b in zip(sums, terms)]
            own_sum[j, c, :, :PIX] = sums[0]
            own_sum[j, c, :, PIX:] = sums[1]
            next_sum[j, c, :, :PIX] = sums[2]
            next_sum[j, c, :, PIX:] = sums[3]
        next_copy(j).start()

    def finish_slice(j):
        next_copy(j).wait_recv()
        for c, target in ((0, new_real), (1, new_imag)):
            target[j] = objects[c][j] - OBJ_STEP * (own_sum[j, c] + next_recv[j, c])

    gather_slice(2)

    wait_got(parts_recv, part_send_sem, part_recv_sem, ring_peer, ring)
    total = parts_recv[0]
    for i in range(1, ring):
        total = total + parts_recv[i]
    line[...] = total
    line_recv[row_of] = total
    start_all(line_copy, n_line)

    gather_slice(1)

    wait_got(line_recv, line_send_sem, line_recv_sem, line_peer, n_line)
    total = line_recv[0]
    for i in range(1, n_line):
        total = total + line_recv[i]
    line_recv[n_line] = total
    cross_recv[depth] = line_recv[n_line, depth]
    start_all(cross_copy, n_depth)
    wait_got(cross_recv, cross_send_sem, cross_recv_sem, depth_peer, n_depth)
    total = cross_recv[0]
    for i in range(1, n_depth):
        total = total + cross_recv[i]
    cross_recv[n_depth] = total
    final[spot] = total
    start_all(final_copy, ring)

    gather_slice(0)
    finish_slice(2)
    finish_slice(1)
    wait_got(final, final_send_sem, final_recv_sem, ring_peer, ring)
    live_total = lax.fori_loop(0, n_tile, lambda i, acc: acc + count_ref[i], 0).astype(jnp.float32)
    rows = pl.ds(pl.multiple_of(depth * quarter, quarter), quarter)
    for c, source, target in ((0, probe_real, new_probe_real), (1, probe_imag, new_probe_imag)):
        for m in range(2):
            for i in range(0, quarter, 8):
                flat = (c * 2 + m) * quarter + i
                grad = final[flat // height, flat % height : flat % height + 8]
                start = pl.multiple_of(depth * quarter + i, 8)
                target[m, i : i + 8] = source[m, pl.ds(start, 8)] - PROBE_STEP * grad / live_total
    finish_slice(0)

    for j in range(GROUP):
        for c in range(2):
            head_copy(j, c).wait_send()
        lax.fori_loop(1, n_depth, lambda i, c, j=j: (patch_copy(j, depth_peer(i)).wait_send(), c)[1], 0)
        next_copy(j).wait_send()

    def piece_sent(k, carry):
        @pl.when(k // GROUP != depth)
        def _():
            piece_copy(k).wait_send()

        return carry

    lax.fori_loop(0, SLICES, piece_sent, 0)
    wait_sent(part_copy, ring)
    wait_sent(line_copy, n_line)
    wait_sent(cross_copy, n_depth)
    wait_sent(final_copy, ring)


def body(
    object_real, object_imag, probe_real, probe_imag, measured, row_offset, col_offset, counts
):
    n_tile, n_depth = lax.axis_size("tile"), lax.axis_size("depth")
    ring = RING if n_tile % RING == 0 else 2
    n_line = n_tile // ring
    slab = object_real.shape
    cols = slab[2]
    height = PIX // ring
    vmem = pl.BlockSpec(memory_space=pltpu.VMEM)
    smem = pl.BlockSpec(memory_space=pltpu.SMEM)
    f32 = jnp.float32
    dma = pltpu.SemaphoreType.DMA
    return pl.pallas_call(
        functools.partial(kernel, n_tile, n_depth, ring),
        out_shape=(
            jax.ShapeDtypeStruct(slab, f32),
            jax.ShapeDtypeStruct(slab, f32),
            jax.ShapeDtypeStruct((2, PIX // n_depth, PIX), f32),
            jax.ShapeDtypeStruct((2, PIX // n_depth, PIX), f32),
        ),
        in_specs=[smem] * 3 + [vmem] * 9,
        out_specs=(vmem,) * 4,
        scratch_shapes=[
            pltpu.VMEM((GROUP, 2, PIX, cols), f32),
            pltpu.VMEM((GROUP, n_depth, 2, PIX, PIX), f32),
            pltpu.VMEM((SLICES, 2, PIX, PIX), f32),
            pltpu.VMEM((SLICES + 1, 2, 2, PIX, PIX), f32),
            pltpu.VMEM((SLICES, 2, PIX, PIX), f32),
            pltpu.VMEM((GROUP, n_depth, 2, PIX, PIX), f32),
            pltpu.VMEM((GROUP, 2, PIX, cols), f32),
            pltpu.VMEM((GROUP, 2, PIX, cols), f32),
            pltpu.VMEM((GROUP, 2, PIX, cols), f32),
            pltpu.VMEM((ring, n_depth, height, PIX), f32),
            pltpu.VMEM((ring, n_depth, height, PIX), f32),
            pltpu.VMEM((n_depth, height, PIX), f32),
            pltpu.VMEM((n_line + 1, n_depth, height, PIX), f32),
            pltpu.VMEM((n_depth + 1, height, PIX), f32),
            pltpu.VMEM((ring, height, PIX), f32),
            dma((GROUP, 2)), dma((GROUP, 2)), dma((GROUP, n_depth)), dma((SLICES,)),
            dma((SLICES,)), dma((GROUP, n_depth)), dma((GROUP,)), dma((GROUP,)),
            dma((ring,)), dma((ring,)), dma((n_line,)), dma((n_line,)),
            dma((n_depth,)), dma((n_depth,)), dma((ring,)), dma((ring,)),
        ],
        compiler_params=pltpu.CompilerParams(
            collective_id=0, has_side_effects=True, vmem_limit_bytes=44 * 1024 * 1024
        ),
    )(
        row_offset, col_offset, counts, object_real, object_imag, probe_real, probe_imag, measured,
        *[jnp.asarray(c) for c in make_constants()],
    )


def solution(mesh):
    placed = (
        P("depth", "tile", None),
        P("depth", "tile", None),
        P(),
        P(),
        P("tile", None, None),
        P("tile"),
        P("tile"),
        P(),
    )
    return jax.shard_map(
        body,
        mesh=mesh,
        in_specs=placed,
        out_specs=(
            P("depth", "tile", None),
            P("depth", "tile", None),
            P(None, "depth", None),
            P(None, "depth", None),
        ),
        check_vma=False,
    )
```

time: 327 us -> 88.1 us (0.27)
  the two profiles are of different devices: /device:TPU:8 before, /device:TPU:36 now
where the time goes in v2:
time: 88.1 us; the launch traced here: 87.7 us
  Pallas kernels  73.6 us (84%)
  local copies, waits for them, and re-layouts  13.4 us (15%)
    pallas_call x1, Pallas kernels, body(): pl.pallas_call(functools.partial(kernel, n_tile, n_depth, ring), out_shap...  73.6 us
    unnamed x28, local copies, waits for them, and re-layouts  13.4 us

profile of v2, /device:TPU:36, one launch (start us, length us, event | category | flops | bytes accessed | tf_op | source)
XLA Modules:
  0.0 87.7 jit_solution(9205608366393882487)
XLA Ops:
  0.6 0.0 copy-start
  0.6 1.0 %copy-done = f32[3,128,256]{2,1,0:T(8,128)S(1)} copy-done((f32[3,128,256]{2,1,0:T(8,128)S(1)}, f32[3,128,256]{2,1,0:T(8,128)}, u32[]{:S(2)}) %copy-start) | copy-done | bytes 393240
  1.6 0.0 copy-start.1
  1.6 1.0 %copy-done.1 = f32[3,128,256]{2,1,0:T(8,128)S(1)} copy-done((f32[3,128,256]{2,1,0:T(8,128)S(1)}, f32[3,128,256]{2,1,0:T(8,128)}, u32[]{:S(2)}) %copy-start.1) | copy-done | bytes 393240
  2.6 0.0 copy-start.2
  2.6 1.0 %copy-done.2 = bf16[256,768]{1,0:T(8,128)(2,1)S(1)} copy-done((bf16[256,768]{1,0:T(8,128)(2,1)S(1)}, bf16[256,768]{1,0:T(8,128)(2,1)}, u32[]{:S(2)}) %copy-start.2) | copy-done | bytes 393240
  3.6 0.0 copy-start.3
  3.6 1.0 %copy-done.3 = bf16[768,256]{1,0:T(8,128)(2,1)S(1)} copy-done((bf16[768,256]{1,0:T(8,128)(2,1)S(1)}, bf16[768,256]{1,0:T(8,128)(2,1)}, u32[]{:S(2)}) %copy-start.3) | copy-done | bytes 393240
  4.6 0.0 copy-start.4
  4.6 1.0 %copy-done.4 = bf16[256,768]{1,0:T(8,128)(2,1)S(1)} copy-done((bf16[256,768]{1,0:T(8,128)(2,1)S(1)}, bf16[256,768]{1,0:T(8,128)(2,1)}, u32[]{:S(2)}) %copy-start.4) | copy-done | bytes 393240
  5.6 0.0 copy-start.5
  5.6 1.0 %copy-done.5 = bf16[768,256]{1,0:T(8,128)(2,1)S(1)} copy-done((bf16[768,256]{1,0:T(8,128)(2,1)S(1)}, bf16[768,256]{1,0:T(8,128)(2,1)}, u32[]{:S(2)}) %copy-start.5) | copy-done | bytes 393240
  6.6 0.0 copy-start.6
  6.6 0.9 %copy-done.6 = f32[4,128,128]{2,1,0:T(8,128)S(1)} copy-done((f32[4,128,128]{2,1,0:T(8,128)S(1)}, f32[4,128,128]{2,1,0:T(8,128)}, u32[]{:S(2)}) %copy-start.6) | copy-done | bytes 262168
  7.6 0.0 copy-start.7
  7.6 0.9 %copy-done.7 = f32[2,128,128]{2,1,0:T(8,128)S(1)} copy-done((f32[2,128,128]{2,1,0:T(8,128)S(1)}, f32[2,128,128]{2,1,0:T(8,128)}, u32[]{:S(2)}) %copy-start.7) | copy-done | bytes 131096
  8.5 0.0 copy-start.8
  8.5 0.9 %copy-done.8 = f32[2,128,128]{2,1,0:T(8,128)S(1)} copy-done((f32[2,128,128]{2,1,0:T(8,128)S(1)}, f32[2,128,128]{2,1,0:T(8,128)}, u32[]{:S(2)}) %copy-start.8) | copy-done | bytes 131096
  9.4 0.0 copy-start.9
  9.4 0.7 copy-done.9
  10.0 0.0 copy-start.10
  10.0 0.7 copy-done.10
  10.7 0.0 copy-start.11
  10.7 0.7 copy-done.11
  11.3 73.6 %shard_map.147 = (f32[3,128,256]{2,1,0:T(8,128)S(1)}, f32[3,128,256]{2,1,0:T(8,128)S(1)}, f32[2,32,128]{2,1,0:T(8,128)S(1)}, f32[2,32,128]{2,1,0:T(8,128)S(1)}) custom-call(s32[4]{0:T(128)S(1)} %copy-done.9, s32[4]{0:T(128)S(1)} %copy-done.10, s32[64]{0:T(128)S(1)} %copy-done.11, f32[3,128,256]{2,1,0:T(8,128)S(1)} %copy-done, f32[3,128,256]{2,1,0:T(8,128)S(1)} %copy-done.1, ...), custom_call_target="tpu_custom_call" | custom-call | tf_op jit(solution)/shard_map/pallas_call | solution.py:412
  84.9 0.7 copy.20
  85.7 0.7 copy.21
  86.4 0.6 copy.22
  87.0 0.6 copy.23
Async XLA Ops:
  0.6 1.0 %copy-start = (f32[3,128,256]{2,1,0:T(8,128)S(1)}, f32[3,128,256]{2,1,0:T(8,128)}, u32[]{:S(2)}) copy-start(f32[3,128,256]{2,1,0:T(8,128)} %obj_real.1) | copy-start | bytes 1179652
  1.6 1.0 %copy-start.1 = (f32[3,128,256]{2,1,0:T(8,128)S(1)}, f32[3,128,256]{2,1,0:T(8,128)}, u32[]{:S(2)}) copy-start(f32[3,128,256]{2,1,0:T(8,128)} %obj_imag.1) | copy-start | bytes 1179652
  2.6 1.0 %copy-start.2 = (bf16[256,768]{1,0:T(8,128)(2,1)S(1)}, bf16[256,768]{1,0:T(8,128)(2,1)}, u32[]{:S(2)}) copy-start(bf16[256,768]{1,0:T(8,128)(2,1)} %constant.11.clone.dft_left) | copy-start | bytes 1179652
  3.6 1.0 %copy-start.3 = (bf16[768,256]{1,0:T(8,128)(2,1)S(1)}, bf16[768,256]{1,0:T(8,128)(2,1)}, u32[]{:S(2)}) copy-start(bf16[768,256]{1,0:T(8,128)(2,1)} %constant.10.clone.dft_right) | copy-start | bytes 1179652
  4.6 1.0 %copy-start.4 = (bf16[256,768]{1,0:T(8,128)(2,1)S(1)}, bf16[256,768]{1,0:T(8,128)(2,1)}, u32[]{:S(2)}) copy-start(bf16[256,768]{1,0:T(8,128)(2,1)} %constant.9.clone.step_left) | copy-start | bytes 1179652
  5.6 1.0 %copy-start.5 = (bf16[768,256]{1,0:T(8,128)(2,1)S(1)}, bf16[768,256]{1,0:T(8,128)(2,1)}, u32[]{:S(2)}) copy-start(bf16[768,256]{1,0:T(8,128)(2,1)} %constant.8.clone.step_right) | copy-start | bytes 1179652
  6.6 0.9 %copy-start.6 = (f32[4,128,128]{2,1,0:T(8,128)S(1)}, f32[4,128,128]{2,1,0:T(8,128)}, u32[]{:S(2)}) copy-start(f32[4,128,128]{2,1,0:T(8,128)} %measured_ref.1) | copy-start | bytes 786436
  7.6 0.9 %copy-start.7 = (f32[2,128,128]{2,1,0:T(8,128)S(1)}, f32[2,128,128]{2,1,0:T(8,128)}, u32[]{:S(2)}) copy-start(f32[2,128,128]{2,1,0:T(8,128)} %probe_real.1) | copy-start | bytes 393220
  8.5 0.9 %copy-start.8 = (f32[2,128,128]{2,1,0:T(8,128)S(1)}, f32[2,128,128]{2,1,0:T(8,128)}, u32[]{:S(2)}) copy-start(f32[2,128,128]{2,1,0:T(8,128)} %probe_imag.1) | copy-start | bytes 393220
  9.4 0.7 copy-start.9
  10.0 0.7 copy-start.10
  10.7 0.7 copy-start.11

commit v3 on v2

v3 whole, which is shorter than its diff:
```python
import functools

import jax
import jax.numpy as jnp
import numpy as np
from jax import lax
from jax.experimental import pallas as pl
from jax.experimental.pallas import tpu as pltpu
from jax.sharding import PartitionSpec as P

PIX = 128
SLICES = 12
GROUP = 3
RING = 16
PROP_PHASE = 12.0
AMP_EPS = 0.05
OBJ_STEP = 1.0
PROBE_STEP = 4.0


def make_constants():
    n = np.arange(PIX)
    dft = np.exp(-2j * np.pi * ((n[:, None] * n[None, :]) % PIX) / PIX) / np.sqrt(PIX)
    freq = ((n + PIX // 2) % PIX - PIX // 2) / PIX
    step = np.conj(dft) @ (np.exp(-1j * PROP_PHASE * freq**2)[:, None] * dft)
    return np.stack([step.real, step.imag, dft.real, dft.imag]).astype(np.float32)


def split(value):
    high = value.astype(jnp.bfloat16)
    low = (value - high.astype(jnp.float32)).astype(jnp.bfloat16)
    return high, low


def make_factors(real, imag, right, left):
    for i, line in enumerate(((real, imag), (-imag, real))):
        high, low = split(jnp.concatenate(line, axis=1))
        for n, part in enumerate((high, high, low)):
            right[2 * n * PIX + i * PIX : 2 * n * PIX + (i + 1) * PIX] = part
    for i, line in enumerate(((real, -imag), (imag, real))):
        high, low = split(jnp.concatenate(line, axis=1))
        for n, part in enumerate((high, high, low)):
            left[i * PIX : (i + 1) * PIX, 2 * n * PIX : 2 * (n + 1) * PIX] = part


def sandwich(field, right, left):
    wide = jnp.concatenate(
        [jnp.concatenate([field[0][m], field[1][m]], axis=1) for m in range(2)], axis=0
    )
    high, low = split(wide)
    middle = jnp.dot(
        jnp.concatenate([high, low, high], axis=1), right, preferred_element_type=jnp.float32
    )
    tall = jnp.concatenate(
        [
            jnp.concatenate([middle[:PIX, c * PIX : (c + 1) * PIX], middle[PIX:, c * PIX : (c + 1) * PIX]], axis=1)
            for c in range(2)
        ],
        axis=0,
    )
    high, low = split(tall)
    done = jnp.dot(
        left, jnp.concatenate([high, low, high], axis=0), preferred_element_type=jnp.float32
    )
    return [[done[c * PIX : (c + 1) * PIX, m * PIX : (m + 1) * PIX] for m in range(2)] for c in range(2)]


def times(patch_real, patch_imag, field):
    real = [field[0][m] * patch_real - field[1][m] * patch_imag for m in range(2)]
    imag = [field[0][m] * patch_imag + field[1][m] * patch_real for m in range(2)]
    return [real, imag]


MESH = pl.DeviceIdType.MESH


def turned(block, rows, cols):
    return pltpu.roll(pltpu.roll(block, rows, 0), cols, 1)


def kernel(
    n_tile, n_depth, ring,
    row_hbm, col_hbm, count_hbm, real_hbm, imag_hbm, probe_real_hbm, probe_imag_hbm, measured_hbm,
    table_hbm,
    new_real, new_imag, new_probe_real, new_probe_imag,
    head, stage, patch_ref, waves, piece_stage, grads, own_sum, next_sum, next_recv,
    parts, core_recv, column, column_recv, plane, plane_recv, final,
    row_ref, col_ref, count_ref, obj_real, obj_imag, probe_real, probe_imag, measured_ref,
    step_right, step_left, dft_right, dft_left, table, load_sem, new_probe, store_sem,
    head_send_sem, head_recv_sem, patch_send_sem, patch_recv_sem, piece_send_sem, grad_recv_sem,
    next_send_sem, next_recv_sem,
    core_sem, column_send_sem, column_recv_sem, plane_send_sem, plane_recv_sem, final_send_sem, final_recv_sem,
):
    objects = (obj_real, obj_imag)
    sources = (real_hbm, imag_hbm)
    tile = lax.axis_index("tile")
    depth = lax.axis_index("depth")

    def fetch(n, src, dst):
        copy = pltpu.make_async_copy(src, dst, load_sem.at[n])
        copy.start()
        return copy

    offset_loads = [fetch(0, row_hbm, row_ref), fetch(1, col_hbm, col_ref)]
    object_loads = [fetch(2, real_hbm, obj_real), fetch(3, imag_hbm, obj_imag)]
    probe_loads = [fetch(4, probe_real_hbm, probe_real), fetch(5, probe_imag_hbm, probe_imag)]
    table_loads = [fetch(6, table_hbm, table)]
    far_loads = [fetch(7, measured_hbm.at[depth], measured_ref), fetch(8, count_hbm, count_ref)]

    def loaded(copies):
        for copy in copies:
            copy.wait()

    after, before = lax.rem(tile + 1, n_tile), lax.rem(tile + n_tile - 1, n_tile)
    n_line = n_tile // ring
    spot, row_of = lax.rem(tile, ring), tile // ring
    ring_base = row_of * ring

    def send(src, dst, send_sem, recv_sem, to_tile, to_depth):
        return pltpu.make_async_remote_copy(
            src_ref=src, dst_ref=dst, send_sem=send_sem, recv_sem=recv_sem,
            device_id=(to_tile, to_depth), device_id_type=MESH,
        )

    def ring_peer(i):
        return lax.rem(spot + i, ring)

    plane_spot = row_of * n_depth + depth

    def plane_peer(i):
        return lax.rem(plane_spot + i, n_line * n_depth)

    def plane_device(n):
        return (n // n_depth) * ring + spot, lax.rem(n, n_depth)

    core, column_spot, n_column = lax.rem(spot, 2), spot // 2, ring // 2

    def column_peer(i):
        return lax.rem(column_spot + i, n_column)

    def depth_peer(i):
        return lax.rem(depth + i, n_depth)

    barrier = pltpu.get_barrier_semaphore()

    def greet(to_tile, to_depth):
        pl.semaphore_signal(barrier, inc=1, device_id=(to_tile, to_depth), device_id_type=MESH)

    greet(after, depth)
    greet(before, depth)
    lax.fori_loop(1, ring, lambda i, c: (greet(ring_base + ring_peer(i), depth), c)[1], 0)
    lax.fori_loop(1, n_line * n_depth, lambda i, c: (greet(*plane_device(plane_peer(i))), c)[1], 0)
    pl.semaphore_wait(barrier, 2 + ring - 1 + n_line * n_depth - 1)

    def head_copy(j, c):
        return send(sources[c].at[j], head.at[j, c], head_send_sem.at[j, c], head_recv_sem.at[j, c], before, depth)

    def start_head(j):
        for c in range(2):
            head_copy(j, c).start()

    start_head(0)

    row_iota = lax.broadcasted_iota(jnp.int32, (PIX, PIX), 0)
    col_iota = lax.broadcasted_iota(jnp.int32, (PIX, PIX), 1)

    def patch_copy(j, to):
        k = depth * GROUP + j
        return send(
            stage.at[j, to], patch_ref.at[k], patch_send_sem.at[j, to], patch_recv_sem.at[k], tile, to
        )

    def each_patch_send(j, act):
        for i in (2, 1, 3):
            act(patch_copy(j, depth_peer(i)))

    def start(copy):
        copy.start()

    def wait_send(copy):
        copy.wait_send()

    def cut(j, i):
        slot = depth_peer(i)
        row, col = row_ref[slot], col_ref[slot]
        own_row, left_col = row_iota >= row, col_iota >= col
        out = []
        for c in range(2):
            upper = jnp.where(left_col, objects[c][j, :, :PIX], objects[c][j, :, PIX:])
            lower = jnp.where(left_col, head[j, c, :, :PIX], head[j, c, :, PIX:])
            block = jnp.where(own_row, upper, lower)
            out.append(turned(block, lax.rem(PIX - row, PIX), lax.rem(PIX - col + PIX, PIX)))
        return slot, out

    def cut_slice(j, carry):
        for c in range(2):
            head_copy(j, c).wait_recv()

        @pl.when(j + 1 < GROUP)
        def _():
            start_head(j + 1)

        def cut_slot(i, carry):
            slot, out = cut(j, i)
            for c in range(2):
                stage[j, slot, c] = out[c]
            return carry

        lax.fori_loop(1, n_depth, cut_slot, 0)

        each_patch_send(j, start)
        _, out = cut(j, 0)
        for c in range(2):
            patch_ref[depth * GROUP + j, c] = out[c]
        return carry

    loaded(offset_loads)
    loaded(object_loads)
    lax.fori_loop(0, GROUP, cut_slice, 0)

    def load(ref, k):
        return [[ref[k, c, m] for m in range(2)] for c in range(2)]

    def store(ref, k, field):
        for c in range(2):
            for m in range(2):
                ref[k, c, m] = field[c][m]

    def patch_ready(k):
        @pl.when(k // GROUP != depth)
        def _():
            send(stage.at[0, 0], patch_ref.at[k], patch_send_sem.at[0, 0], patch_recv_sem.at[k], tile, depth).wait_recv()

    loaded(probe_loads)
    loaded(table_loads)
    make_factors(table[0], table[1], step_right, step_left)
    make_factors(table[2], table[3], dft_right, dft_left)
    store(waves, 0, [[probe_real[m] for m in range(2)], [probe_imag[m] for m in range(2)]])

    def forward(k, carry):
        patch_ready(k)

        chi = times(patch_ref[k, 0], patch_ref[k, 1], load(waves, k))
        store(waves, k + 1, sandwich(chi, step_right[...], step_left[...]))
        return carry

    last = SLICES - 1
    lax.fori_loop(0, last, forward, 0)
    patch_ready(last)
    loaded(far_loads)
    exit_wave = times(patch_ref[last, 0], patch_ref[last, 1], load(waves, last))
    far = sandwich(exit_wave, dft_right[...], dft_left[...])
    intensity = sum(far[c][m] * far[c][m] for c in range(2) for m in range(2))
    live = jnp.where(depth < count_ref[tile], 1.0, 0.0)
    factor = (1.0 - measured_ref[...] * lax.rsqrt(intensity + AMP_EPS)) * live
    bent = [[far[0][m] * factor for m in range(2)], [-far[1][m] * factor for m in range(2)]]
    store(waves, SLICES, sandwich(bent, dft_right[...], dft_left[...]))

    own_turn = (row_ref[depth], col_ref[depth])

    def collect(k, grad):
        wave = load(waves, k)
        real = sum(wave[0][m] * grad[0][m] - wave[1][m] * grad[1][m] for m in range(2))
        imag = -sum(wave[0][m] * grad[1][m] + wave[1][m] * grad[0][m] for m in range(2))
        row, col = own_turn
        piece_stage[k, 0] = turned(real, row, lax.rem(col, PIX))
        piece_stage[k, 1] = turned(imag, row, lax.rem(col, PIX))
        return times(patch_ref[k, 0], patch_ref[k, 1], grad)

    def piece_copy(k):
        j = lax.rem(k, GROUP)
        return send(
            piece_stage.at[k], grads.at[j, depth], piece_send_sem.at[k], grad_recv_sem.at[j, depth], tile, k // GROUP
        )

    def deliver(k):
        here = k // GROUP == depth

        @pl.when(jnp.logical_and(jnp.logical_not(here), k > 1))
        def _():
            piece_copy(k).start()

        @pl.when(here)
        def _():
            grads[lax.rem(k, GROUP), depth] = piece_stage[k]

    def release(k):
        @pl.when(depth != 0)
        def _():
            piece_copy(k + 1).wait_send()
            piece_copy(k).start()

    def backward(i, carry):
        k = last - i
        bent = collect(k, load(waves, SLICES))
        store(waves, SLICES, sandwich(bent, step_right[...], step_left[...]))
        deliver(k)
        return carry

    lax.fori_loop(0, last, backward, 0)
    entry = collect(0, load(waves, SLICES))
    deliver(0)

    quarter = PIX // n_depth
    height = 4 * quarter // ring
    for c in range(2):
        for m in range(2):
            value = entry[c][m] if c == 0 else -entry[c][m]
            for d in range(n_depth):
                for i in range(0, quarter, 8):
                    flat = (c * 2 + m) * quarter + i
                    part = flat // height
                    parts[part % 2, part // 2, d, flat % height : flat % height + 8] = value[
                        d * quarter + i : d * quarter + i + 8
                    ]

    core_copy = send(parts.at[1 - core], core_recv, core_sem.at[0], core_sem.at[1], tile + 1 - 2 * core, depth)

    def column_copy(i):
        to = column_peer(i)
        return send(
            column.at[to], column_recv.at[column_spot], column_send_sem.at[to], column_recv_sem.at[column_spot],
            ring_base + 2 * to + core, depth,
        )

    def plane_copy(i):
        to = plane_peer(i)
        to_tile, to_depth = plane_device(to)
        return send(
            plane.at[to_depth], plane_recv.at[plane_spot], plane_send_sem.at[to], plane_recv_sem.at[plane_spot],
            to_tile, to_depth,
        )

    def final_copy(i):
        to = ring_peer(i)
        return send(
            final.at[spot], final.at[spot], final_send_sem.at[to], final_recv_sem.at[spot],
            ring_base + to, depth,
        )

    def start_all(copy, count):
        lax.fori_loop(1, count, lambda i, c: (copy(i).start(), c)[1], 0)

    def wait_sent(copy, count):
        lax.fori_loop(1, count, lambda i, c: (copy(i).wait_send(), c)[1], 0)

    def wait_got(buffer, send_sem, recv_sem, peer, count):
        def one(i, carry):
            frm = peer(i)
            send(buffer.at[frm], buffer.at[frm], send_sem.at[frm], recv_sem.at[frm], tile, depth).wait_recv()
            return carry

        lax.fori_loop(1, count, one, 0)

    def next_copy(j):
        return send(next_sum.at[j], next_recv.at[j], next_send_sem.at[j], next_recv_sem.at[j], after, depth)

    def gather_slice(j):
        def arrived(i, carry):
            frm = depth_peer(i)
            sem = grad_recv_sem.at[j, frm]
            send(grads.at[j, frm], grads.at[j, frm], sem, sem, tile, depth).wait_recv()
            return carry

        lax.fori_loop(1, n_depth, arrived, 0)
        for c in range(2):
            sums = [0.0] * 4
            for slot in range(n_depth):
                own_row, left_col = row_iota >= row_ref[slot], col_iota >= col_ref[slot]
                block = grads[j, slot, c]
                upper = jnp.where(own_row, block, 0.0)
                lower = block - upper
                upper_left = jnp.where(left_col, upper, 0.0)
                lower_left = jnp.where(left_col, lower, 0.0)
                terms = (upper_left, upper - upper_left, lower_left, lower - lower_left)
                sums = [a + b for a, b in zip(sums, terms)]
            own_sum[j, c, :, :PIX] = sums[0]
            own_sum[j, c, :, PIX:] = sums[1]
            next_sum[j, c, :, :PIX] = sums[2]
            next_sum[j, c, :, PIX:] = sums[3]
        next_copy(j).start()

    def object_store(j, c):
        return pltpu.make_async_copy(own_sum.at[j, c], (new_real, new_imag)[c].at[j], store_sem.at[j, c])

    def probe_store(c):
        return pltpu.make_async_copy(new_probe.at[c], (new_probe_real, new_probe_imag)[c], store_sem.at[GROUP, c])

    def finish_slice(j):
        next_copy(j).wait_recv()
        for c in range(2):
            own_sum[j, c] = objects[c][j] - OBJ_STEP * (own_sum[j, c] + next_recv[j, c])
            object_store(j, c).start()

    core_copy.start()
    core_copy.wait_recv()
    for n in range(n_column):
        column[n] = parts[core, n] + core_recv[n]
    column_recv[column_spot] = column[column_spot]
    start_all(column_copy, n_column)
    release(1)
    gather_slice(2)

    wait_got(column_recv, column_send_sem, column_recv_sem, column_peer, n_column)
    total = column_recv[0]
    for i in range(1, n_column):
        total = total + column_recv[i]
    plane[...] = total
    plane_recv[plane_spot] = plane[depth]
    start_all(plane_copy, n_line * n_depth)
    release(0)

    gather_slice(1)

    wait_got(plane_recv, plane_send_sem, plane_recv_sem, plane_peer, n_line * n_depth)
    total = plane_recv[0]
    for i in range(1, n_line * n_depth):
        total = total + plane_recv[i]
    final[spot] = total
    start_all(final_copy, ring)

    gather_slice(0)
    finish_slice(2)
    finish_slice(1)
    wait_got(final, final_send_sem, final_recv_sem, ring_peer, ring)
    live_total = lax.fori_loop(0, n_tile, lambda i, acc: acc + count_ref[i], 0).astype(jnp.float32)
    for c, source in ((0, probe_real), (1, probe_imag)):
        for m in range(2):
            for i in range(0, quarter, 8):
                flat = (c * 2 + m) * quarter + i
                grad = final[flat // height, flat % height : flat % height + 8]
                start = pl.multiple_of(depth * quarter + i, 8)
                new_probe[c, m, i : i + 8] = source[m, pl.ds(start, 8)] - PROBE_STEP * grad / live_total
        probe_store(c).start()
    finish_slice(0)

    for j in range(GROUP):
        for c in range(2):
            head_copy(j, c).wait_send()
        each_patch_send(j, wait_send)

        next_copy(j).wait_send()

    def piece_sent(k, carry):
        @pl.when(jnp.logical_and(k // GROUP != depth, jnp.logical_or(k == 0, k >= GROUP)))
        def _():
            piece_copy(k).wait_send()

        return carry

    lax.fori_loop(0, SLICES, piece_sent, 0)
    for c in range(2):
        for j in range(GROUP):
            object_store(j, c).wait()
        probe_store(c).wait()
    core_copy.wait_send()
    wait_sent(column_copy, n_column)
    wait_sent(plane_copy, n_line * n_depth)
    wait_sent(final_copy, ring)


def hand_over(*refs):
    sources, targets, held, load_sem, store_sem = refs[:4], refs[4:8], refs[8:12], refs[12], refs[13]
    chunks = []
    for i in range(4):
        for n in range(sources[i].shape[0]):
            at = (i, n)
            chunks.append((
                pltpu.make_async_copy(sources[i].at[n], held[i].at[n], load_sem.at[at]),
                pltpu.make_async_copy(held[i].at[n], targets[i].at[n], store_sem.at[at]),
            ))
    for load, _ in chunks:
        load.start()
    for load, store in chunks:
        load.wait()
        store.start()
    for _, store in chunks:
        store.wait()


def body(
    object_real, object_imag, probe_real, probe_imag, measured, row_offset, col_offset, counts
):
    n_tile, n_depth = lax.axis_size("tile"), lax.axis_size("depth")
    ring = min(RING, n_tile // 2)
    n_line = n_tile // ring
    slab = object_real.shape
    cols = slab[2]
    height = PIX // ring
    hbm = pl.BlockSpec(memory_space=pltpu.HBM)
    smem = pltpu.SMEM
    f32 = jnp.float32
    dma = pltpu.SemaphoreType.DMA
    results = pl.pallas_call(
        functools.partial(kernel, n_tile, n_depth, ring),
        out_shape=(
            jax.ShapeDtypeStruct(slab, f32),
            jax.ShapeDtypeStruct(slab, f32),
            jax.ShapeDtypeStruct((2, PIX // n_depth, PIX), f32),
            jax.ShapeDtypeStruct((2, PIX // n_depth, PIX), f32),
        ),
        in_specs=[hbm] * 9,
        out_specs=(hbm,) * 4,
        scratch_shapes=[
            pltpu.VMEM((GROUP, 2, PIX, cols), f32),
            pltpu.VMEM((GROUP, n_depth, 2, PIX, PIX), f32),
            pltpu.VMEM((SLICES, 2, PIX, PIX), f32),
            pltpu.VMEM((SLICES + 1, 2, 2, PIX, PIX), f32),
            pltpu.VMEM((SLICES, 2, PIX, PIX), f32),
            pltpu.VMEM((GROUP, n_depth, 2, PIX, PIX), f32),
            pltpu.VMEM((GROUP, 2, PIX, cols), f32),
            pltpu.VMEM((GROUP, 2, PIX, cols), f32),
            pltpu.VMEM((GROUP, 2, PIX, cols), f32),
            pltpu.VMEM((2, ring // 2, n_depth, height, PIX), f32),
            pltpu.VMEM((ring // 2, n_depth, height, PIX), f32),
            pltpu.VMEM((ring // 2, n_depth, height, PIX), f32),
            pltpu.VMEM((ring // 2, n_depth, height, PIX), f32),
            pltpu.VMEM((n_depth, height, PIX), f32),
            pltpu.VMEM((n_line * n_depth, height, PIX), f32),
            pltpu.VMEM((ring, height, PIX), f32),
            smem(row_offset.shape, jnp.int32), smem(col_offset.shape, jnp.int32), smem(counts.shape, jnp.int32),
            pltpu.VMEM(slab, f32), pltpu.VMEM(slab, f32),
            pltpu.VMEM(probe_real.shape, f32), pltpu.VMEM(probe_real.shape, f32),
            pltpu.VMEM(measured.shape[1:], f32),
            *[pltpu.VMEM(s, jnp.bfloat16) for s in ((6 * PIX, 2 * PIX), (2 * PIX, 6 * PIX))] * 2,
            pltpu.VMEM((4, PIX, PIX), f32), dma((9,)),
            pltpu.VMEM((2, 2, PIX // n_depth, PIX), f32), dma((GROUP + 1, 2)),
            dma((GROUP, 2)), dma((GROUP, 2)), dma((GROUP, n_depth)), dma((SLICES,)),
            dma((SLICES,)), dma((GROUP, n_depth)), dma((GROUP,)), dma((GROUP,)),
            dma((2,)), dma((ring // 2,)), dma((ring // 2,)),
            dma((n_line * n_depth,)), dma((n_line * n_depth,)), dma((ring,)), dma((ring,)),
        ],
        compiler_params=pltpu.CompilerParams(
            collective_id=0, has_side_effects=True, vmem_limit_bytes=60 * 1024 * 1024
        ),
    )(
        row_offset, col_offset, counts, object_real, object_imag, probe_real, probe_imag, measured,
        jnp.asarray(make_constants()),
    )
    return pl.pallas_call(
        hand_over,
        out_shape=tuple(jax.ShapeDtypeStruct(r.shape, r.dtype) for r in results),
        in_specs=[hbm] * 4,
        out_specs=(hbm,) * 4,
        scratch_shapes=[pltpu.VMEM(r.shape, r.dtype) for r in results] + [dma((4, GROUP)), dma((4, GROUP))],
        compiler_params=pltpu.CompilerParams(vmem_limit_bytes=60 * 1024 * 1024),
    )(*results)


def solution(mesh):
    placed = (
        P("depth", "tile", None),
        P("depth", "tile", None),
        P(),
        P(),
        P("tile", None, None),
        P("tile"),
        P("tile"),
        P(),
    )
    return jax.shard_map(
        body,
        mesh=mesh,
        in_specs=placed,
        out_specs=(
            P("depth", "tile", None),
            P("depth", "tile", None),
            P(None, "depth", None),
            P(None, "depth", None),
        ),
        check_vma=False,
    )
```

time: 88.1 us -> 78.4 us (0.89)
  the two profiles are of different devices: /device:TPU:36 before, /device:TPU:8 now
where the time goes in v3:
time: 78.4 us; the launch traced here: 77.8 us
  Pallas kernels  77.2 us (98%)
    pallas_call x1, Pallas kernels, body(): pl.pallas_call(functools.partial(kernel, n_tile, n_depth, ring), out_shap...  75.1 us
    pallas_call x1, Pallas kernels, body(): pl.pallas_call(hand_over, out_shape=tuple((jax.ShapeDtypeStruct(r.shape,...  2.08 us

profile of v3, /device:TPU:8, one launch (start us, length us, event | category | flops | bytes accessed | tf_op | source)
XLA Modules:
  0.0 77.8 jit_solution(4140689832764748801)
XLA Ops:
  0.6 75.1 %shard_map.120 = (f32[3,128,256]{2,1,0:T(8,128)}, f32[3,128,256]{2,1,0:T(8,128)}, f32[2,32,128]{2,1,0:T(8,128)}, f32[2,32,128]{2,1,0:T(8,128)}) custom-call(s32[4]{0:T(128)} %row_hbm.1, s32[4]{0:T(128)} %col_hbm.1, s32[64]{0:T(128)} %count_hbm.1, f32[3,128,256]{2,1,0:T(8,128)} %real_hbm.1, f32[3,128,256]{2,1,0:T(8,128)} %imag_hbm.1, ...), custom_call_target="tpu_custom_call" | custom-call | tf_op jit(solution)/shard_map/pallas_call | solution.py:494
  75.7 2.1 %shard_map.121 = (f32[3,128,256]{2,1,0:T(8,128)}, f32[3,128,256]{2,1,0:T(8,128)}, f32[2,32,128]{2,1,0:T(8,128)}, f32[2,32,128]{2,1,0:T(8,128)}) custom-call(f32[3,128,256]{2,1,0:T(8,128)} %get-tuple-element.8.refs_0_, f32[3,128,256]{2,1,0:T(8,128)} %get-tuple-element.9.refs_1_, f32[2,32,128]{2,1,0:T(8,128)} %get-tuple-element.10.refs_2_, ...), custom_call_target="tpu_custom_call" | custom-call | tf_op jit(solution)/shard_map/pallas_call | solution.py:540

commit v4 on v3

--- a/solution.py
+++ b/solution.py
@@ -44,25 +44,17 @@
 
 
 def sandwich(field, right, left):
-    wide = jnp.concatenate(
-        [jnp.concatenate([field[0][m], field[1][m]], axis=1) for m in range(2)], axis=0
-    )
-    high, low = split(wide)
-    middle = jnp.dot(
-        jnp.concatenate([high, low, high], axis=1), right, preferred_element_type=jnp.float32
-    )
-    tall = jnp.concatenate(
-        [
-            jnp.concatenate([middle[:PIX, c * PIX : (c + 1) * PIX], middle[PIX:, c * PIX : (c + 1) * PIX]], axis=1)
-            for c in range(2)
-        ],
-        axis=0,
-    )
-    high, low = split(tall)
-    done = jnp.dot(
-        left, jnp.concatenate([high, low, high], axis=0), preferred_element_type=jnp.float32
-    )
-    return [[done[c * PIX : (c + 1) * PIX, m * PIX : (m + 1) * PIX] for m in range(2)] for c in range(2)]
+    middle = []
+    for m in range(2):
+        high, low = split(jnp.concatenate([field[0][m], field[1][m]], axis=1))
+        wide = jnp.concatenate([high, low, high], axis=1)
+        middle.append(jnp.dot(wide, right, preferred_element_type=jnp.float32))
+    done = []
+    for m in range(2):
+        high, low = split(jnp.concatenate([middle[m][:, :PIX], middle[m][:, PIX:]], axis=0))
+        tall = jnp.concatenate([high, low, high], axis=0)
+        done.append(jnp.dot(left, tall, preferred_element_type=jnp.float32))
+    return [[done[m][c * PIX : (c + 1) * PIX] for m in range(2)] for c in range(2)]
 
 
 def times(patch_real, patch_imag, field):
@@ -90,6 +82,7 @@
     head_send_sem, head_recv_sem, patch_send_sem, patch_recv_sem, piece_send_sem, grad_recv_sem,
     next_send_sem, next_recv_sem,
     core_sem, column_send_sem, column_recv_sem, plane_send_sem, plane_recv_sem, final_send_sem, final_recv_sem,
+    last_send_sem, last_recv_sem, relay, half_send_sem, half_recv_sem, in_send_sem, in_recv_sem, out_send_sem,
 ):
     objects = (obj_real, obj_imag)
     sources = (real_hbm, imag_hbm)
@@ -273,22 +266,67 @@
             piece_stage.at[k], grads.at[j, depth], piece_send_sem.at[k], grad_recv_sem.at[j, depth], tile, k // GROUP
         )
 
+    def last_copy(c):
+        return send(
+            piece_stage.at[0, c], grads.at[0, depth, c], last_send_sem.at[c], last_recv_sem.at[depth, c], tile, 0
+        )
+
+    def half_copy():
+        return send(
+            piece_stage.at[1, 0], grads.at[1, depth, 0], half_send_sem.at[0], half_recv_sem.at[0], tile, 0
+        )
+
+    def relay_in_copy(j):
+        return send(piece_stage.at[j, 1], relay.at[j], in_send_sem.at[j], in_recv_sem.at[j], tile, 1)
+
+    def relay_out_copy(j):
+        sem = last_recv_sem.at[2, 1] if j == 0 else half_recv_sem.at[1]
+        return send(relay.at[j], grads.at[j, 2, 1], out_send_sem.at[j], sem, tile, 0)
+
+    def start_piece(k):
+        @pl.when(k // GROUP != depth)
+        def _():
+            piece_copy(k).start()
+
+    def start_piece_one():
+        @pl.when(lax.rem(depth, 2) == 1)
+        def _():
+            piece_copy(1).start()
+
+        @pl.when(depth == 2)
+        def _():
+            half_copy().start()
+            relay_in_copy(1).start()
+
+    def start_last(c):
+        @pl.when(lax.rem(depth, 2) == 1)
+        def _():
+            last_copy(c).start()
+
+    def start_last_of_two():
+        @pl.when(depth == 2)
+        def _():
+            last_copy(0).start()
+            relay_in_copy(0).start()
+
+    def pass_on(j):
+        @pl.when(depth == 1)
+        def _():
+            relay_in_copy(j).wait_recv()
+            relay_out_copy(j).start()
+
     def deliver(k):
-        here = k // GROUP == depth
-
-        @pl.when(jnp.logical_and(jnp.logical_not(here), k > 1))
-        def _():
-            piece_copy(k).start()
-
-        @pl.when(here)
+        @pl.when(k // GROUP == depth)
         def _():
             grads[lax.rem(k, GROUP), depth] = piece_stage[k]
 
-    def release(k):
-        @pl.when(depth != 0)
-        def _():
-            piece_copy(k + 1).wait_send()
-            piece_copy(k).start()
+        @pl.when(lax.rem(k, GROUP) == GROUP - 1)
+        def _():
+            start_piece(k)
+
+        @pl.when(k == 4)
+        def _():
+            start_piece(10)
 
     def backward(i, carry):
         k = last - i
@@ -352,33 +390,73 @@
 
         lax.fori_loop(1, count, one, 0)
 
-    def next_copy(j):
-        return send(next_sum.at[j], next_recv.at[j], next_send_sem.at[j], next_recv_sem.at[j], after, depth)
+    def next_copy(j, c):
+        return send(
+            next_sum.at[j, c], next_recv.at[j, c], next_send_sem.at[j, c], next_recv_sem.at[j, c], after, depth
+        )
+
+    def arrived(j, i):
+        frm = depth_peer(i)
+        sem = grad_recv_sem.at[j, frm]
+        send(grads.at[j, frm], grads.at[j, frm], sem, sem, tile, depth).wait_recv()
+
+    def half_arrived(c, i):
+        frm = depth_peer(i)
+        sem = last_recv_sem.at[frm, c]
+        send(grads.at[0, frm, c], grads.at[0, frm, c], sem, sem, tile, depth).wait_recv()
+
+    def gather_half(j, c):
+        sums = [0.0] * 4
+        for slot in range(n_depth):
+            own_row, left_col = row_iota >= row_ref[slot], col_iota >= col_ref[slot]
+            block = grads[j, slot, c]
+            upper = jnp.where(own_row, block, 0.0)
+            lower = block - upper
+            upper_left = jnp.where(left_col, upper, 0.0)
+            lower_left = jnp.where(left_col, lower, 0.0)
+            terms = (upper_left, upper - upper_left, lower_left, lower - lower_left)
+            sums = [a + b for a, b in zip(sums, terms)]
+        own_sum[j, c, :, :PIX] = sums[0]
+        own_sum[j, c, :, PIX:] = sums[1]
+        next_sum[j, c, :, :PIX] = sums[2]
+        next_sum[j, c, :, PIX:] = sums[3]
+        next_copy(j, c).start()
 
     def gather_slice(j):
-        def arrived(i, carry):
-            frm = depth_peer(i)
-            sem = grad_recv_sem.at[j, frm]
-            send(grads.at[j, frm], grads.at[j, frm], sem, sem, tile, depth).wait_recv()
+        if j == 2:
+            for i in range(1, n_depth):
+                arrived(j, i)
+        elif j == 1:
+            arrived(j, 1)
+            arrived(j, 3)
+
+            @pl.when(depth == 0)
+            def _():
+                for c in range(2):
+                    sem, half = half_recv_sem.at[c], grads.at[1, 2, c]
+                    send(half, half, sem, sem, tile, depth).wait_recv()
+
+            @pl.when(depth != 0)
+            def _():
+                arrived(j, 2)
+
+        else:
+            @pl.when(depth != 0)
+            def _():
+                for i in range(1, n_depth):
+                    arrived(j, i)
+
+        def half(c, carry):
+            if j == 0:
+                @pl.when(depth == 0)
+                def _():
+                    for i in range(1, n_depth):
+                        half_arrived(c, i)
+
+            gather_half(j, c)
             return carry
 
-        lax.fori_loop(1, n_depth, arrived, 0)
-        for c in range(2):
-            sums = [0.0] * 4
-            for slot in range(n_depth):
-                own_row, left_col = row_iota >= row_ref[slot], col_iota >= col_ref[slot]
-                block = grads[j, slot, c]
-                upper = jnp.where(own_row, block, 0.0)
-                lower = block - upper
-                upper_left = jnp.where(left_col, upper, 0.0)
-                lower_left = jnp.where(left_col, lower, 0.0)
-                terms = (upper_left, upper - upper_left, lower_left, lower - lower_left)
-                sums = [a + b for a, b in zip(sums, terms)]
-            own_sum[j, c, :, :PIX] = sums[0]
-            own_sum[j, c, :, PIX:] = sums[1]
-            next_sum[j, c, :, :PIX] = sums[2]
-            next_sum[j, c, :, PIX:] = sums[3]
-        next_copy(j).start()
+        lax.fori_loop(0, 2, half, 0)
 
     def object_store(j, c):
         return pltpu.make_async_copy(own_sum.at[j, c], (new_real, new_imag)[c].at[j], store_sem.at[j, c])
@@ -387,18 +465,21 @@
         return pltpu.make_async_copy(new_probe.at[c], (new_probe_real, new_probe_imag)[c], store_sem.at[GROUP, c])
 
     def finish_slice(j):
-        next_copy(j).wait_recv()
-        for c in range(2):
+        for c in range(2):
+            next_copy(j, c).wait_recv()
             own_sum[j, c] = objects[c][j] - OBJ_STEP * (own_sum[j, c] + next_recv[j, c])
             object_store(j, c).start()
 
     core_copy.start()
+    start_piece(7)
     core_copy.wait_recv()
     for n in range(n_column):
         column[n] = parts[core, n] + core_recv[n]
     column_recv[column_spot] = column[column_spot]
     start_all(column_copy, n_column)
-    release(1)
+    for k in (9, 4):
+        start_piece(k)
+    start_piece_one()
     gather_slice(2)
 
     wait_got(column_recv, column_send_sem, column_recv_sem, column_peer, n_column)
@@ -408,8 +489,11 @@
     plane[...] = total
     plane_recv[plane_spot] = plane[depth]
     start_all(plane_copy, n_line * n_depth)
-    release(0)
-
+    for k in (6, 3):
+        start_piece(k)
+    start_last(0)
+    start_last_of_two()
+    pass_on(1)
     gather_slice(1)
 
     wait_got(plane_recv, plane_send_sem, plane_recv_sem, plane_peer, n_line * n_depth)
@@ -418,7 +502,8 @@
         total = total + plane_recv[i]
     final[spot] = total
     start_all(final_copy, ring)
-
+    start_last(1)
+    pass_on(0)
     gather_slice(0)
     finish_slice(2)
     finish_slice(1)
@@ -439,16 +524,36 @@
             head_copy(j, c).wait_send()
         each_patch_send(j, wait_send)
 
-        next_copy(j).wait_send()
+        for c in range(2):
+            next_copy(j, c).wait_send()
 
     def piece_sent(k, carry):
-        @pl.when(jnp.logical_and(k // GROUP != depth, jnp.logical_or(k == 0, k >= GROUP)))
+        @pl.when(k // GROUP != depth)
         def _():
             piece_copy(k).wait_send()
 
         return carry
 
-    lax.fori_loop(0, SLICES, piece_sent, 0)
+    lax.fori_loop(2, SLICES, piece_sent, 0)
+
+    @pl.when(lax.rem(depth, 2) == 1)
+    def _():
+        piece_copy(1).wait_send()
+        last_copy(0).wait_send()
+        last_copy(1).wait_send()
+
+    @pl.when(depth == 2)
+    def _():
+        half_copy().wait_send()
+        last_copy(0).wait_send()
+        relay_in_copy(0).wait_send()
+        relay_in_copy(1).wait_send()
+
+    @pl.when(depth == 1)
+    def _():
+        relay_out_copy(0).wait_send()
+        relay_out_copy(1).wait_send()
+
     for c in range(2):
         for j in range(GROUP):
             object_store(j, c).wait()
@@ -526,9 +631,11 @@
             pltpu.VMEM((4, PIX, PIX), f32), dma((9,)),
             pltpu.VMEM((2, 2, PIX // n_depth, PIX), f32), dma((GROUP + 1, 2)),
             dma((GROUP, 2)), dma((GROUP, 2)), dma((GROUP, n_depth)), dma((SLICES,)),
-            dma((SLICES,)), dma((GROUP, n_depth)), dma((GROUP,)), dma((GROUP,)),
+            dma((SLICES,)), dma((GROUP, n_depth)), dma((GROUP, 2)), dma((GROUP, 2)),
             dma((2,)), dma((ring // 2,)), dma((ring // 2,)),
             dma((n_line * n_depth,)), dma((n_line * n_depth,)), dma((ring,)), dma((ring,)),
+            dma((2,)), dma((n_depth, 2)), pltpu.VMEM((2, PIX, PIX), f32),
+            dma((1,)), dma((2,)), dma((2,)), dma((2,)), dma((2,)),
         ],
         compiler_params=pltpu.CompilerParams(
             collective_id=0, has_side_effects=True, vmem_limit_bytes=60 * 1024 * 1024

time: 78.4 us -> 75.9 us (0.968)
  Pallas kernels: 77.2 us -> 75.1 us
    pallas_call x1, Pallas kernels: 75.1 us -> 73 us  [body(): pl.pallas_call(functools.partial(kernel, n_tile, n_depth, ring), out_shap...]
where the time goes in v4:
time: 75.9 us; the launch traced here: 75.8 us
  Pallas kernels  75.1 us (99%)
    pallas_call x1, Pallas kernels, body(): pl.pallas_call(functools.partial(kernel, n_tile, n_depth, ring), out_shap...  73 us
    pallas_call x1, Pallas kernels, body(): pl.pallas_call(hand_over, out_shape=tuple((jax.ShapeDtypeStruct(r.shape,...  2.08 us

profile of v4, /device:TPU:8, one launch (start us, length us, event | category | flops | bytes accessed | tf_op | source)
XLA Modules:
  0.0 75.8 jit_solution(1269136775524966881)
XLA Ops:
  0.6 73.0 %shard_map.120 = (f32[3,128,256]{2,1,0:T(8,128)}, f32[3,128,256]{2,1,0:T(8,128)}, f32[2,32,128]{2,1,0:T(8,128)}, f32[2,32,128]{2,1,0:T(8,128)}) custom-call(s32[4]{0:T(128)} %row_hbm.1, s32[4]{0:T(128)} %col_hbm.1, s32[64]{0:T(128)} %count_hbm.1, f32[3,128,256]{2,1,0:T(8,128)} %real_hbm.1, f32[3,128,256]{2,1,0:T(8,128)} %imag_hbm.1, ...), custom_call_target="tpu_custom_call" | custom-call | tf_op jit(solution)/shard_map/pallas_call | solution.py:599
  73.7 2.1 %shard_map.121 = (f32[3,128,256]{2,1,0:T(8,128)}, f32[3,128,256]{2,1,0:T(8,128)}, f32[2,32,128]{2,1,0:T(8,128)}, f32[2,32,128]{2,1,0:T(8,128)}) custom-call(f32[3,128,256]{2,1,0:T(8,128)} %get-tuple-element.8.refs_0_, f32[3,128,256]{2,1,0:T(8,128)} %get-tuple-element.9.refs_1_, f32[2,32,128]{2,1,0:T(8,128)} %get-tuple-element.10.refs_2_, ...), custom_call_target="tpu_custom_call" | custom-call | tf_op jit(solution)/shard_map/pallas_call | solution.py:647

commit v5 on v4

--- a/solution.py
+++ b/solution.py
@@ -89,6 +89,45 @@
     tile = lax.axis_index("tile")
     depth = lax.axis_index("depth")
 
+    after, before = lax.rem(tile + 1, n_tile), lax.rem(tile + n_tile - 1, n_tile)
+    n_line = n_tile // ring
+    spot, row_of = lax.rem(tile, ring), tile // ring
+    ring_base = row_of * ring
+
+    def send(src, dst, send_sem, recv_sem, to_tile, to_depth):
+        return pltpu.make_async_remote_copy(
+            src_ref=src, dst_ref=dst, send_sem=send_sem, recv_sem=recv_sem,
+            device_id=(to_tile, to_depth), device_id_type=MESH,
+        )
+
+    def ring_peer(i):
+        return lax.rem(spot + i, ring)
+
+    plane_spot = row_of * n_depth + depth
+
+    def plane_peer(i):
+        return lax.rem(plane_spot + i, n_line * n_depth)
+
+    def plane_device(n):
+        return (n // n_depth) * ring + spot, lax.rem(n, n_depth)
+
+    core, column_spot, n_column = lax.rem(spot, 2), spot // 2, ring // 2
+
+    def column_peer(i):
+        return lax.rem(column_spot + i, n_column)
+
+    def depth_peer(i):
+        return lax.rem(depth + i, n_depth)
+
+    barrier = pltpu.get_barrier_semaphore()
+
+    def greet(to_tile, to_depth):
+        pl.semaphore_signal(barrier, inc=1, device_id=(to_tile, to_depth), device_id_type=MESH)
+
+    greet(after, depth)
+    greet(before, depth)
+    lax.fori_loop(1, ring, lambda i, c: (greet(ring_base + ring_peer(i), depth), c)[1], 0)
+    lax.fori_loop(1, n_line * n_depth, lambda i, c: (greet(*plane_device(plane_peer(i))), c)[1], 0)
     def fetch(n, src, dst):
         copy = pltpu.make_async_copy(src, dst, load_sem.at[n])
         copy.start()
@@ -104,45 +143,6 @@
         for copy in copies:
             copy.wait()
 
-    after, before = lax.rem(tile + 1, n_tile), lax.rem(tile + n_tile - 1, n_tile)
-    n_line = n_tile // ring
-    spot, row_of = lax.rem(tile, ring), tile // ring
-    ring_base = row_of * ring
-
-    def send(src, dst, send_sem, recv_sem, to_tile, to_depth):
-        return pltpu.make_async_remote_copy(
-            src_ref=src, dst_ref=dst, send_sem=send_sem, recv_sem=recv_sem,
-            device_id=(to_tile, to_depth), device_id_type=MESH,
-        )
-
-    def ring_peer(i):
-        return lax.rem(spot + i, ring)
-
-    plane_spot = row_of * n_depth + depth
-
-    def plane_peer(i):
-        return lax.rem(plane_spot + i, n_line * n_depth)
-
-    def plane_device(n):
-        return (n // n_depth) * ring + spot, lax.rem(n, n_depth)
-
-    core, column_spot, n_column = lax.rem(spot, 2), spot // 2, ring // 2
-
-    def column_peer(i):
-        return lax.rem(column_spot + i, n_column)
-
-    def depth_peer(i):
-        return lax.rem(depth + i, n_depth)
-
-    barrier = pltpu.get_barrier_semaphore()
-
-    def greet(to_tile, to_depth):
-        pl.semaphore_signal(barrier, inc=1, device_id=(to_tile, to_depth), device_id_type=MESH)
-
-    greet(after, depth)
-    greet(before, depth)
-    lax.fori_loop(1, ring, lambda i, c: (greet(ring_base + ring_peer(i), depth), c)[1], 0)
-    lax.fori_loop(1, n_line * n_depth, lambda i, c: (greet(*plane_device(plane_peer(i))), c)[1], 0)
     pl.semaphore_wait(barrier, 2 + ring - 1 + n_line * n_depth - 1)
 
     def head_copy(j, c):
@@ -157,54 +157,34 @@
     row_iota = lax.broadcasted_iota(jnp.int32, (PIX, PIX), 0)
     col_iota = lax.broadcasted_iota(jnp.int32, (PIX, PIX), 1)
 
-    def patch_copy(j, to):
+    def patch_copy(j, c, to):
         k = depth * GROUP + j
         return send(
-            stage.at[j, to], patch_ref.at[k], patch_send_sem.at[j, to], patch_recv_sem.at[k], tile, to
-        )
-
-    def each_patch_send(j, act):
-        for i in (2, 1, 3):
-            act(patch_copy(j, depth_peer(i)))
-
-    def start(copy):
-        copy.start()
-
-    def wait_send(copy):
-        copy.wait_send()
-
-    def cut(j, i):
+            stage.at[j, to, c], patch_ref.at[k, c], patch_send_sem.at[j, to, c], patch_recv_sem.at[k, c], tile, to
+        )
+
+    def cut(j, c, i):
         slot = depth_peer(i)
         row, col = row_ref[slot], col_ref[slot]
         own_row, left_col = row_iota >= row, col_iota >= col
-        out = []
-        for c in range(2):
-            upper = jnp.where(left_col, objects[c][j, :, :PIX], objects[c][j, :, PIX:])
-            lower = jnp.where(left_col, head[j, c, :, :PIX], head[j, c, :, PIX:])
-            block = jnp.where(own_row, upper, lower)
-            out.append(turned(block, lax.rem(PIX - row, PIX), lax.rem(PIX - col + PIX, PIX)))
-        return slot, out
+        upper = jnp.where(left_col, objects[c][j, :, :PIX], objects[c][j, :, PIX:])
+        lower = jnp.where(left_col, head[j, c, :, :PIX], head[j, c, :, PIX:])
+        block = jnp.where(own_row, upper, lower)
+        return turned(block, lax.rem(PIX - row, PIX), lax.rem(PIX - col + PIX, PIX))
 
     def cut_slice(j, carry):
         for c in range(2):
             head_copy(j, c).wait_recv()
-
-        @pl.when(j + 1 < GROUP)
-        def _():
-            start_head(j + 1)
-
-        def cut_slot(i, carry):
-            slot, out = cut(j, i)
-            for c in range(2):
-                stage[j, slot, c] = out[c]
-            return carry
-
-        lax.fori_loop(1, n_depth, cut_slot, 0)
-
-        each_patch_send(j, start)
-        _, out = cut(j, 0)
-        for c in range(2):
-            patch_ref[depth * GROUP + j, c] = out[c]
+            if c == 1:
+                @pl.when(j + 1 < GROUP)
+                def _():
+                    start_head(j + 1)
+
+            for i in (2, 1, 3):
+                slot = depth_peer(i)
+                stage[j, slot, c] = cut(j, c, i)
+                patch_copy(j, c, slot).start()
+            patch_ref[depth * GROUP + j, c] = cut(j, c, 0)
         return carry
 
     loaded(offset_loads)
@@ -222,7 +202,9 @@
     def patch_ready(k):
         @pl.when(k // GROUP != depth)
         def _():
-            send(stage.at[0, 0], patch_ref.at[k], patch_send_sem.at[0, 0], patch_recv_sem.at[k], tile, depth).wait_recv()
+            for c in range(2):
+                sem = patch_recv_sem.at[k, c]
+                send(stage.at[0, 0, 0], patch_ref.at[k, c], sem, sem, tile, depth).wait_recv()
 
     loaded(probe_loads)
     loaded(table_loads)
@@ -471,15 +453,14 @@
             object_store(j, c).start()
 
     core_copy.start()
-    start_piece(7)
+    start_piece_one()
     core_copy.wait_recv()
     for n in range(n_column):
         column[n] = parts[core, n] + core_recv[n]
     column_recv[column_spot] = column[column_spot]
     start_all(column_copy, n_column)
-    for k in (9, 4):
+    for k in (4, 7, 9):
         start_piece(k)
-    start_piece_one()
     gather_slice(2)
 
     wait_got(column_recv, column_send_sem, column_recv_sem, column_peer, n_column)
@@ -489,11 +470,11 @@
     plane[...] = total
     plane_recv[plane_spot] = plane[depth]
     start_all(plane_copy, n_line * n_depth)
-    for k in (6, 3):
-        start_piece(k)
     start_last(0)
     start_last_of_two()
     pass_on(1)
+    for k in (3, 6):
+        start_piece(k)
     gather_slice(1)
 
     wait_got(plane_recv, plane_send_sem, plane_recv_sem, plane_peer, n_line * n_depth)
@@ -522,7 +503,9 @@
     for j in range(GROUP):
         for c in range(2):
             head_copy(j, c).wait_send()
-        each_patch_send(j, wait_send)
+        for i in range(1, n_depth):
+            for c in range(2):
+                patch_copy(j, c, depth_peer(i)).wait_send()
 
         for c in range(2):
             next_copy(j, c).wait_send()
@@ -630,7 +613,7 @@
             *[pltpu.VMEM(s, jnp.bfloat16) for s in ((6 * PIX, 2 * PIX), (2 * PIX, 6 * PIX))] * 2,
             pltpu.VMEM((4, PIX, PIX), f32), dma((9,)),
             pltpu.VMEM((2, 2, PIX // n_depth, PIX), f32), dma((GROUP + 1, 2)),
-            dma((GROUP, 2)), dma((GROUP, 2)), dma((GROUP, n_depth)), dma((SLICES,)),
+            dma((GROUP, 2)), dma((GROUP, 2)), dma((GROUP, n_depth, 2)), dma((SLICES, 2)),
             dma((SLICES,)), dma((GROUP, n_depth)), dma((GROUP, 2)), dma((GROUP, 2)),
             dma((2,)), dma((ring // 2,)), dma((ring // 2,)),
             dma((n_line * n_depth,)), dma((n_line * n_depth,)), dma((ring,)), dma((ring,)),

time: 75.9 us -> 74.6 us (0.983)
  Pallas kernels: 75.1 us -> 73.8 us
    pallas_call x1, Pallas kernels: 73 us -> 71.7 us  [body(): pl.pallas_call(functools.partial(kernel, n_tile, n_depth, ring), out_shap...]
where the time goes in v5:
time: 74.6 us; the launch traced here: 74.5 us
  Pallas kernels  73.8 us (99%)
    pallas_call x1, Pallas kernels, body(): pl.pallas_call(functools.partial(kernel, n_tile, n_depth, ring), out_shap...  71.7 us
    pallas_call x1, Pallas kernels, body(): pl.pallas_call(hand_over, out_shape=tuple((jax.ShapeDtypeStruct(r.shape,...  2.08 us

profile of v5, /device:TPU:8, one launch (start us, length us, event | category | flops | bytes accessed | tf_op | source)
XLA Modules:
  0.0 74.5 jit_solution(10348370389066427764)
XLA Ops:
  0.6 71.7 %shard_map.120 = (f32[3,128,256]{2,1,0:T(8,128)}, f32[3,128,256]{2,1,0:T(8,128)}, f32[2,32,128]{2,1,0:T(8,128)}, f32[2,32,128]{2,1,0:T(8,128)}) custom-call(s32[4]{0:T(128)} %row_hbm.1, s32[4]{0:T(128)} %col_hbm.1, s32[64]{0:T(128)} %count_hbm.1, f32[3,128,256]{2,1,0:T(8,128)} %real_hbm.1, f32[3,128,256]{2,1,0:T(8,128)} %imag_hbm.1, ...), custom_call_target="tpu_custom_call" | custom-call | tf_op jit(solution)/shard_map/pallas_call | solution.py:582
  72.4 2.1 %shard_map.121 = (f32[3,128,256]{2,1,0:T(8,128)}, f32[3,128,256]{2,1,0:T(8,128)}, f32[2,32,128]{2,1,0:T(8,128)}, f32[2,32,128]{2,1,0:T(8,128)}) custom-call(f32[3,128,256]{2,1,0:T(8,128)} %get-tuple-element.8.refs_0_, f32[3,128,256]{2,1,0:T(8,128)} %get-tuple-element.9.refs_1_, f32[2,32,128]{2,1,0:T(8,128)} %get-tuple-element.10.refs_2_, ...), custom_call_target="tpu_custom_call" | custom-call | tf_op jit(solution)/shard_map/pallas_call | solution.py:630

commit v6 on v5

--- a/solution.py
+++ b/solution.py
@@ -461,6 +461,13 @@
     start_all(column_copy, n_column)
     for k in (4, 7, 9):
         start_piece(k)
+    for j in range(GROUP):
+        for c in range(2):
+            head_copy(j, c).wait_send()
+        for i in range(1, n_depth):
+            for c in range(2):
+                patch_copy(j, c, depth_peer(i)).wait_send()
+
     gather_slice(2)
 
     wait_got(column_recv, column_send_sem, column_recv_sem, column_peer, n_column)
@@ -488,8 +495,42 @@
     gather_slice(0)
     finish_slice(2)
     finish_slice(1)
+    for j in (2, 1):
+        for c in range(2):
+            next_copy(j, c).wait_send()
+
+    def piece_sent(k, carry):
+        @pl.when(k // GROUP != depth)
+        def _():
+            piece_copy(k).wait_send()
+
+        return carry
+
+    lax.fori_loop(2, SLICES, piece_sent, 0)
+
+    @pl.when(lax.rem(depth, 2) == 1)
+    def _():
+        piece_copy(1).wait_send()
+        last_copy(0).wait_send()
+        last_copy(1).wait_send()
+
+    @pl.when(depth == 2)
+    def _():
+        half_copy().wait_send()
+        last_copy(0).wait_send()
+        relay_in_copy(0).wait_send()
+        relay_in_copy(1).wait_send()
+
+    @pl.when(depth == 1)
+    def _():
+        relay_out_copy(0).wait_send()
+        relay_out_copy(1).wait_send()
+
+    core_copy.wait_send()
+    wait_sent(column_copy, n_column)
+    wait_sent(plane_copy, n_line * n_depth)
+    live_total = lax.fori_loop(0, n_tile, lambda i, acc: acc + count_ref[i], 0).astype(jnp.float32)
     wait_got(final, final_send_sem, final_recv_sem, ring_peer, ring)
-    live_total = lax.fori_loop(0, n_tile, lambda i, acc: acc + count_ref[i], 0).astype(jnp.float32)
     for c, source in ((0, probe_real), (1, probe_imag)):
         for m in range(2):
             for i in range(0, quarter, 8):
@@ -499,52 +540,13 @@
                 new_probe[c, m, i : i + 8] = source[m, pl.ds(start, 8)] - PROBE_STEP * grad / live_total
         probe_store(c).start()
     finish_slice(0)
-
-    for j in range(GROUP):
-        for c in range(2):
-            head_copy(j, c).wait_send()
-        for i in range(1, n_depth):
-            for c in range(2):
-                patch_copy(j, c, depth_peer(i)).wait_send()
-
-        for c in range(2):
-            next_copy(j, c).wait_send()
-
-    def piece_sent(k, carry):
-        @pl.when(k // GROUP != depth)
-        def _():
-            piece_copy(k).wait_send()
-
-        return carry
-
-    lax.fori_loop(2, SLICES, piece_sent, 0)
-
-    @pl.when(lax.rem(depth, 2) == 1)
-    def _():
-        piece_copy(1).wait_send()
-        last_copy(0).wait_send()
-        last_copy(1).wait_send()
-
-    @pl.when(depth == 2)
-    def _():
-        half_copy().wait_send()
-        last_copy(0).wait_send()
-        relay_in_copy(0).wait_send()
-        relay_in_copy(1).wait_send()
-
-    @pl.when(depth == 1)
-    def _():
-        relay_out_copy(0).wait_send()
-        relay_out_copy(1).wait_send()
-
+    for c in range(2):
+        next_copy(0, c).wait_send()
+    wait_sent(final_copy, ring)
     for c in range(2):
         for j in range(GROUP):
             object_store(j, c).wait()
         probe_store(c).wait()
-    core_copy.wait_send()
-    wait_sent(column_copy, n_column)
-    wait_sent(plane_copy, n_line * n_depth)
-    wait_sent(final_copy, ring)
 
 
 def hand_over(*refs):

time: 74.6 us -> 74.2 us (level)
  no operation moved by 1% of the time
where the time goes in v6:
time: 74.2 us; the launch traced here: 74.1 us
  Pallas kernels  73.4 us (99%)
    pallas_call x1, Pallas kernels, body(): pl.pallas_call(functools.partial(kernel, n_tile, n_depth, ring), out_shap...  71.3 us
    pallas_call x1, Pallas kernels, body(): pl.pallas_call(hand_over, out_shape=tuple((jax.ShapeDtypeStruct(r.shape,...  2.08 us

profile of v6, /device:TPU:8, one launch (start us, length us, event | category | flops | bytes accessed | tf_op | source)
XLA Modules:
  0.0 74.1 jit_solution(6313241916981719265)
XLA Ops:
  0.6 71.3 %shard_map.120 = (f32[3,128,256]{2,1,0:T(8,128)}, f32[3,128,256]{2,1,0:T(8,128)}, f32[2,32,128]{2,1,0:T(8,128)}, f32[2,32,128]{2,1,0:T(8,128)}) custom-call(s32[4]{0:T(128)} %row_hbm.1, s32[4]{0:T(128)} %col_hbm.1, s32[64]{0:T(128)} %count_hbm.1, f32[3,128,256]{2,1,0:T(8,128)} %real_hbm.1, f32[3,128,256]{2,1,0:T(8,128)} %imag_hbm.1, ...), custom_call_target="tpu_custom_call" | custom-call | tf_op jit(solution)/shard_map/pallas_call | solution.py:584
  72.0 2.1 %shard_map.121 = (f32[3,128,256]{2,1,0:T(8,128)}, f32[3,128,256]{2,1,0:T(8,128)}, f32[2,32,128]{2,1,0:T(8,128)}, f32[2,32,128]{2,1,0:T(8,128)}) custom-call(f32[3,128,256]{2,1,0:T(8,128)} %get-tuple-element.8.refs_0_, f32[3,128,256]{2,1,0:T(8,128)} %get-tuple-element.9.refs_1_, f32[2,32,128]{2,1,0:T(8,128)} %get-tuple-element.10.refs_2_, ...), custom_call_target="tpu_custom_call" | custom-call | tf_op jit(solution)/shard_map/pallas_call | solution.py:632

commit v7 on v6

--- a/solution.py
+++ b/solution.py
@@ -483,6 +483,7 @@
     for k in (3, 6):
         start_piece(k)
     gather_slice(1)
+    start_last(1)
 
     wait_got(plane_recv, plane_send_sem, plane_recv_sem, plane_peer, n_line * n_depth)
     total = plane_recv[0]
@@ -490,7 +491,6 @@
         total = total + plane_recv[i]
     final[spot] = total
     start_all(final_copy, ring)
-    start_last(1)
     pass_on(0)
     gather_slice(0)
     finish_slice(2)

time: 74.2 us -> 74.2 us (level)
  no operation moved by 1% of the time
where the time goes in v7:
time: 74.2 us; the launch traced here: 74.1 us
  Pallas kernels  73.4 us (99%)
    pallas_call x1, Pallas kernels, body(): pl.pallas_call(functools.partial(kernel, n_tile, n_depth, ring), out_shap...  71.3 us
    pallas_call x1, Pallas kernels, body(): pl.pallas_call(hand_over, out_shape=tuple((jax.ShapeDtypeStruct(r.shape,...  2.08 us

profile of v7, /device:TPU:8, one launch (start us, length us, event | category | flops | bytes accessed | tf_op | source)
XLA Modules:
  0.0 74.1 jit_solution(16401696628316778267)
XLA Ops:
  0.6 71.3 %shard_map.120 = (f32[3,128,256]{2,1,0:T(8,128)}, f32[3,128,256]{2,1,0:T(8,128)}, f32[2,32,128]{2,1,0:T(8,128)}, f32[2,32,128]{2,1,0:T(8,128)}) custom-call(s32[4]{0:T(128)} %row_hbm.1, s32[4]{0:T(128)} %col_hbm.1, s32[64]{0:T(128)} %count_hbm.1, f32[3,128,256]{2,1,0:T(8,128)} %real_hbm.1, f32[3,128,256]{2,1,0:T(8,128)} %imag_hbm.1, ...), custom_call_target="tpu_custom_call" | custom-call | tf_op jit(solution)/shard_map/pallas_call | solution.py:584
  72.0 2.1 %shard_map.121 = (f32[3,128,256]{2,1,0:T(8,128)}, f32[3,128,256]{2,1,0:T(8,128)}, f32[2,32,128]{2,1,0:T(8,128)}, f32[2,32,128]{2,1,0:T(8,128)}) custom-call(f32[3,128,256]{2,1,0:T(8,128)} %get-tuple-element.8.refs_0_, f32[3,128,256]{2,1,0:T(8,128)} %get-tuple-element.9.refs_1_, f32[2,32,128]{2,1,0:T(8,128)} %get-tuple-element.10.refs_2_, ...), custom_call_target="tpu_custom_call" | custom-call | tf_op jit(solution)/shard_map/pallas_call | solution.py:632
